TPU v7x, 512 devices: a whole 4x8x8 slice. The times are simulated.
512 devices in a mesh: seg: 16 (over z, core), chan: 32 (over y, x).
Axes of the slice: x: 4, y: 8, z: 8, core: 2. Of those that a mesh axis runs over, the one named last changes fastest.
Arguments:
- das_records: float32 [16384, 8, 1500], P(('seg', 'chan')), may hold values from -6 to 6
- source_ids: int32 [4, 2], replicated, may hold values from 0 to 16383
- near_pairs: int32 [65536, 2], P(('seg', 'chan')), may hold values from 0 to 16383, as said below
- pair_count: int32 [512], P(('seg', 'chan')), may hold values from 64 to 128, as said below
Outputs:
- source_xcorr: float32 [4, 2, 16384, 256], P(None, None, ('seg', 'chan'))
- pair_xcorr: float32 [65536, 256], P(('seg', 'chan'))
Inputs may be any that keep to these rules, and one draw needn't show every extreme that they name: `near_pairs`: every slot, live or not, holds valid channels: the first lies in the block of 32 channels of the slot's device, the second 1 to 8 channels away from it; the offset 8 occurs on every device. `pair_count`: some device has all 128 slots live.
All inputs are finite; a program needn't handle non-finite values.
Results may differ from a plain program's by a relative error of at most 0.0003.
Values sent between devices are 32-bit elements; how exact they have to be, the bound alone decides.
A program may use at most 64 MiB of HBM per device.

v0:
```python
import math

import jax
import jax.numpy as jnp
from jax import lax
from jax.sharding import PartitionSpec as P

WIN = 8
L = 1500
FLO = 30
NB = 512
SMOOTH = 4
LAGS = 256
ROUNDS = 4


clip_level = 2.0
water_level = 0.1
epsilon = 1e-06


def broadcast(value, axis, source):
    kept = jnp.where(lax.axis_index(axis) == source, value, 0).astype(value.dtype)
    return lax.psum(kept, axis)


def passed_along(array, axis, by):
    count = lax.axis_size(axis)
    pairs = [(i, i + by) for i in range(count) if 0 <= i + by < count]
    return lax.ppermute(array, axis, pairs)


def normalize(records):
    centered = records - jnp.mean(records, axis=-1, keepdims=True)
    root_mean = jnp.sqrt(jnp.mean(centered * centered, axis=-1, keepdims=True) + epsilon)
    return jnp.clip(centered / root_mean, -clip_level, clip_level)


def whiten(spectrum):
    real_part = spectrum[..., :NB]
    imag_part = spectrum[..., NB:]
    amplitude = jnp.sqrt(real_part * real_part + imag_part * imag_part)
    widths = [(0, 0)] * (amplitude.ndim - 1) + [(SMOOTH, SMOOTH)]
    padded = jnp.pad(amplitude, widths, mode="edge")
    smoothed = padded[..., 0:NB]
    for k in range(1, 2 * SMOOTH + 1):
        smoothed = smoothed + padded[..., k : k + NB]
    denominator = (
        smoothed / (2 * SMOOTH + 1)
        + water_level * jnp.mean(amplitude, axis=-1, keepdims=True)
        + epsilon
    )
    return spectrum / jnp.concatenate([denominator, denominator], axis=-1)


def correlate(left_spec, right_spec):
    left_real, left_imag = (left_spec[..., :NB], left_spec[..., NB:])
    right_real, right_imag = (right_spec[..., :NB], right_spec[..., NB:])
    cross_real = jnp.sum(left_real * right_real + left_imag * right_imag, axis=-2)
    cross_imag = jnp.sum(left_real * right_imag - left_imag * right_real, axis=-2)
    return jnp.concatenate([cross_real, cross_imag], axis=-1)


def band_table():
    sample_idx = jnp.arange(L, dtype=jnp.int32)
    bin_idx = FLO + jnp.arange(NB, dtype=jnp.int32)
    phase_index = sample_idx[:, None] * bin_idx[None, :] % L
    phases = phase_index.astype(jnp.float32) * (2.0 * math.pi / L)
    return jnp.concatenate([jnp.cos(phases), -jnp.sin(phases)], axis=1)


def lag_table():
    bin_idx = FLO + jnp.arange(NB, dtype=jnp.int32)
    lag_idx = jnp.arange(LAGS, dtype=jnp.int32) - LAGS // 2
    phase_index = bin_idx[:, None] * lag_idx[None, :] % L
    phases = phase_index.astype(jnp.float32) * (2.0 * math.pi / L)
    scale = 1.0 / math.sqrt(WIN * NB)
    return jnp.concatenate([jnp.cos(phases), -jnp.sin(phases)], axis=0) * scale


def shards(das_records, source_ids, near_pairs, pair_count):
    precise = lax.Precision.HIGHEST
    ch_count = das_records.shape[0]
    windows = das_records.shape[1]
    normed = normalize(das_records).reshape(ch_count * windows, L)
    spectra = whiten(jnp.dot(normed, band_table(), precision=precise)).reshape(
        ch_count, windows, 2 * NB
    )
    device = lax.axis_index(("seg", "chan"))
    base_channel = device * ch_count
    flat_ids = source_ids.reshape(-1)
    gathered = []
    for slot_num in range(flat_ids.shape[0]):
        source_id = flat_ids[slot_num]
        row_index = jnp.clip(source_id - base_channel, 0, ch_count - 1)
        spectrum_row = lax.dynamic_index_in_dim(spectra, row_index, 0, keepdims=False)
        gathered.append(broadcast(spectrum_row, ("seg", "chan"), source_id // ch_count))
    sources = jnp.stack(gathered)
    inverse = lag_table()
    src_real, src_imag = (sources[..., :NB], sources[..., NB:])
    loc_real, loc_imag = (spectra[..., :NB], spectra[..., NB:])
    cross_real = jnp.einsum("swf,cwf->scf", src_real, loc_real, precision=precise) + jnp.einsum(
        "swf,cwf->scf", src_imag, loc_imag, precision=precise
    )
    cross_imag = jnp.einsum("swf,cwf->scf", src_real, loc_imag, precision=precise) - jnp.einsum(
        "swf,cwf->scf", src_imag, loc_real, precision=precise
    )
    count_src = sources.shape[0]
    cross_spec = jnp.concatenate([cross_real, cross_imag], axis=-1).reshape(
        count_src * ch_count, 2 * NB
    )
    source_xcorr = jnp.dot(cross_spec, inverse, precision=precise).reshape(
        ROUNDS, 2, ch_count, LAGS
    )
    prev_spectra = passed_along(spectra, ("seg", "chan"), 1)
    next_spectra = passed_along(spectra, ("seg", "chan"), -1)
    extended = jnp.concatenate([prev_spectra, spectra, next_spectra], axis=0)
    left_rows = jnp.take(spectra, near_pairs[:, 0] - base_channel, axis=0, mode="clip")
    right_rows = jnp.take(extended, near_pairs[:, 1] - base_channel + ch_count, axis=0, mode="clip")
    pair_result = jnp.dot(correlate(left_rows, right_rows), inverse, precision=precise)
    live_mask = (jnp.arange(near_pairs.shape[0], dtype=jnp.int32) < pair_count[0]).astype(
        jnp.float32
    )
    pair_xcorr = pair_result * live_mask[:, None]
    return (source_xcorr, pair_xcorr)


def solution(mesh):
    in_specs = (P(("seg", "chan"), None, None), P(), P(("seg", "chan"), None), P(("seg", "chan")))
    out_specs = (P(None, None, ("seg", "chan"), None), P(("seg", "chan"), None))
    return jax.shard_map(shards, mesh=mesh, in_specs=in_specs, out_specs=out_specs, check_vma=False)
```

profile of v0, /device:TPU:1, one launch (start us, length us, event | category | flops | bytes accessed | tf_op | source)
XLA Modules:
  0.0 401.9 jit_solution(15392904718365745093)
XLA Ops:
  7.2 14.0 %fusion.8 = (f32[1500,512]{1,0:T(8,128)}, f32[1500,512]{1,0:T(8,128)}) fusion(s32[512]{0:T(512)S(1)} %iota_add_fusion), kind=kLoop, calls=%fused_computation.14 | loop fusion | flops 7680000 | bytes 6146048 | tf_op jit(solution)/shard_map/cos | solution.py:69
  21.7 8.5 %fusion = f32[256,1024]{1,0:T(8,128)S(1)} fusion(f32[1500,512]{1,0:T(8,128)} %get-tuple-element.31, f32[1500,512]{1,0:T(8,128)} %get-tuple-element.30, f32[32,8,1500]{2,1,0:T(8,128)S(1)} %copy-done.4, f32[32,8]{1,0:T(8,128)S(1)} %add_sqrt_fusion, f32[32,8]{1,0:T(8,128)S(1)} %broadcast_multiply_fusion), kind=kOutput, calls=%fused_computation.2 | convolution fusion | flops 4721280000 | bytes 8730624 | tf_op jit(solution)/shard_map/dot_general | solution.py:86
  30.9 1.4 fusion.26
  32.5 8.7 %collective-permute-start.1 = (f32[32,8,1024]{2,1,0:T(8,128)S(1)}, f32[32,8,1024]{2,1,0:T(8,128)}, u32[]{:S(2)}, u32[]{:S(2)}) collective-permute-start(f32[32,8,1024]{2,1,0:T(8,128)S(1)} %fusion.14), channel_id=1, source_target_pairs={{1,0},{2,1},{3,2},{4,3},{5,4},{6,5},{7,6},{8,7},{9,8},{10,9},{11,1... | collective-permute-start | bytes 3145736 | tf_op jit(solution)/shard_map/ppermute | solution.py:30
  41.2 1.9 collective-permute-start
  70.1 3.3 fusion.49
  73.4 2.0 copy.40
  75.4 2.1 copy.38
  77.5 2.8 gather_fusion
  80.9 262.8 %all-reduce.3.cloned.1.call-done = (f32[1,8,1024]{2,1,0:T(8,128)}, f32[1,8,1024]{2,1,0:T(8,128)}, f32[1,8,1024]{2,1,0:T(8,128)}, f32[1,8,1024]{2,1,0:T(8,128)}, ...) async-done(((f32[1,8,1024]{2,1,0:T(8,128)}, f32[1,8,1024]{2,1,0:T(8,128)}, f32[1,8,1024]{2,1,0:T(8,128)}, ...) | async-done | bytes 262160 | tf_op jit(solution)/shard_map/psum | solution.py:24
  343.7 0.8 constant_dynamic-update-slice_fusion.7
  344.5 0.8 constant_dynamic-update-slice_fusion.6
  345.2 0.8 constant_dynamic-update-slice_fusion.5
  346.0 0.8 constant_dynamic-update-slice_fusion.4
  346.8 0.8 constant_dynamic-update-slice_fusion.3
  347.5 0.8 constant_dynamic-update-slice_fusion.2
  348.3 0.8 constant_dynamic-update-slice_fusion.1
  349.0 0.8 constant_dynamic-update-slice_fusion
  349.8 0.7 copy.39
  350.6 2.0 copy.41
  352.6 5.4 %fusion.64 = f32[512,32,8]{1,2,0:T(8,128)S(1)} fusion(f32[32,8,512]{0,1,2:T(8,128)} %copy.40, f32[8,8,512]{1,0,2:T(8,128)S(1)} %copy.39), kind=kOutput, calls=%fused_computation.125 | convolution fusion | flops 12582912 | bytes 1179648 | tf_op jit(solution)/shard_map/swf,cwf->scf/dot_general | solution.py:105
  358.0 4.9 %subtract_bitcast_fusion = f32[8,32,512]{1,0,2:T(8,128)} fusion(f32[512,32,8]{1,2,0:T(8,128)S(1)} %fusion.64, f32[32,8,512]{0,1,2:T(8,128)S(1)} %copy-done.1, f32[8,8,512]{1,0,2:T(8,128)S(1)} %copy-done.2), kind=kOutput, calls=%fused_computation.18 | convolution fusion | flops 12713984 | bytes 1703936 | tf_op jit(solution)/shard_map/swf,cwf->scf/dot_general | solution.py:105
  362.9 3.0 copy.36
  365.9 5.7 %fusion.63 = f32[512,32,8]{1,2,0:T(8,128)S(1)} fusion(f32[32,8,512]{0,1,2:T(8,128)} %copy.38, f32[8,8,512]{1,0,2:T(8,128)S(1)} %copy.39), kind=kOutput, calls=%fused_computation.124 | convolution fusion | flops 12582912 | bytes 1179648 | tf_op jit(solution)/shard_map/swf,cwf->scf/dot_general | solution.py:102
  371.5 3.5 add_bitcast_fusion
  375.1 1.5 copy.35
  376.6 1.4 pad_maximum_fusion.1
  378.1 1.7 fusion.15
  379.8 3.7 pad_maximum_fusion
  383.5 4.7 %gather_fusion.1 = f32[128,8,1024]{2,1,0:T(8,128)} fusion(f32[96,8,1024]{2,1,0:T(8,128)} %pad_maximum_fusion, s32[1024]{0:T(1024)S(1)} %get-tuple-element.42), kind=kCustom, calls=%fused_computation.1 | custom fusion | bytes 8389120 | tf_op jit(solution)/shard_map/jit(_take)/gather | solution.py:119
  388.2 5.5 %add_reduce_fusion = (f32[128,512]{1,0:T(8,128)S(1)}, f32[128,512]{1,0:T(8,128)S(1)}) fusion(f32[128,8,1024]{2,1,0:T(8,128)} %gather_fusion.1, f32[128,8,1024]{2,1,0:T(8,128)} %gather_fusion), kind=kLoop, calls=%fused_computation.17 | loop fusion | flops 4063232 | bytes 8912896 | tf_op jit(solution)/shard_map/reduce_sum | solution.py:59
  393.7 1.3 convolution_multiply_fusion
  (43 shorter events, 3.2 us)
Async XLA Ops:
  7.2 336.6 %all-reduce.3.cloned.1.call-start = ((), (), s32[]{:S(2)}) async-start(), calls=%async_computation | async-start | bytes 524288 | tf_op jit(solution)/shard_map/psum | solution.py:24
  7.2 14.0 %copy-start.4 = (f32[32,8,1500]{2,1,0:T(8,128)S(1)}, f32[32,8,1500]{2,1,0:T(8,128)}, u32[]{:S(2)}) copy-start(f32[32,8,1500]{2,1,0:T(8,128)} %param.4) | copy-start | bytes 4608004
  30.7 12.4 %copy-start.7 = (s32[4,2]{0,1:T(2,128)S(1)}, s32[4,2]{0,1:T(2,128)}, u32[]{:S(2)}) copy-start(s32[4,2]{0,1:T(2,128)} %param.5) | copy-start | bytes 100
  32.5 347.3 %collective-permute-start.1 = (f32[32,8,1024]{2,1,0:T(8,128)S(1)}, f32[32,8,1024]{2,1,0:T(8,128)}, u32[]{:S(2)}, u32[]{:S(2)}) collective-permute-start(f32[32,8,1024]{2,1,0:T(8,128)S(1)} %fusion.14), channel_id=1, source_target_pairs={{1,0},{2,1},{3,2},{4,3},{5,4},{6,5},{7,6},{8,7},{9,8},{10,9},{11,1... | collective-permute-start | bytes 3145736 | tf_op jit(solution)/shard_map/ppermute | solution.py:30
  41.2 338.7 %collective-permute-start = (f32[32,8,1024]{2,1,0:T(8,128)S(1)}, f32[32,8,1024]{2,1,0:T(8,128)}, u32[]{:S(2)}, u32[]{:S(2)}) collective-permute-start(f32[32,8,1024]{2,1,0:T(8,128)S(1)} %fusion.14), channel_id=1, source_target_pairs={{0,1},{1,2},{2,3},{3,4},{4,5},{5,6},{6,7},{7,8},{8,9},{9,10},{10,1... | collective-permute-start | bytes 3145736 | tf_op jit(solution)/shard_map/ppermute | solution.py:30
  63.9 9.4 %copy-start.8 = (s32[128,2]{0,1:T(2,128)S(1)}, s32[128,2]{0,1:T(2,128)}, u32[]{:S(2)}) copy-start(s32[128,2]{0,1:T(2,128)} %param.6) | copy-start | bytes 3076
  352.6 5.4 %copy-start.1 = (f32[32,8,512]{0,1,2:T(8,128)S(1)}, f32[32,8,512]{0,1,2:T(8,128)}, u32[]{:S(2)}) copy-start(f32[32,8,512]{0,1,2:T(8,128)} %copy.38) | copy-start | bytes 1572868
  352.6 5.4 %copy-start.2 = (f32[8,8,512]{1,0,2:T(8,128)S(1)}, f32[8,8,512]{1,0,2:T(8,128)}, u32[]{:S(2)}) copy-start(f32[8,8,512]{1,0,2:T(8,128)} %copy.41) | copy-start | bytes 393220
  365.9 5.7 %copy-start = (f32[32,8,512]{0,1,2:T(8,128)S(1)}, f32[32,8,512]{0,1,2:T(8,128)}, u32[]{:S(2)}) copy-start(f32[32,8,512]{0,1,2:T(8,128)} %copy.40) | copy-start | bytes 1572868
  365.9 5.7 %copy-start.3 = (f32[8,8,512]{1,0,2:T(8,128)S(1)}, f32[8,8,512]{1,0,2:T(8,128)}, u32[]{:S(2)}) copy-start(f32[8,8,512]{1,0,2:T(8,128)} %copy.41) | copy-start | bytes 393220
  376.6 1.4 copy-start.5
  376.6 1.5 copy-start.6
Sparse Core Ops, SparseCore 0:
  70.1 273.5 all-reduce.2
where the time goes:
time: 403 us; the launch traced here: 402 us
  waiting for transfers between devices  263 us (65%)
  between operations  40.2 us (10%)
  matrix products  31 us (8%)
  other arithmetic  30.9 us (8%)
  local copies, waits for them, and re-layouts  26.3 us (7%)
  starting transfers between devices  10.6 us (3%)
    psum x1, waiting for transfers between devices, broadcast(): return lax.psum(kept, axis)  263 us
    cos x1, other arithmetic, band_table(): return jnp.concatenate([jnp.cos(phases), -jnp.sin(phases)], axis=1)  14 us
    unnamed x30, local copies, waits for them, and re-layouts  12.4 us
    ppermute x2, starting transfers between devices, passed_along(): return lax.ppermute(array, axis, pairs)  10.6 us
    dot_general x1, matrix products, shards(): jnp.dot(normed, band_table(), precision=precise)  8.45 us
  transfers between devices with their start and end apart: 3, of which 1 were waited for; matrix products, arithmetic and copies ran while one was open for 12% of the time, Pallas kernels for 0%

commit v1 on v0

v1 whole, which is shorter than its diff:
```python
import functools
import math

import jax
import jax.numpy as jnp
import ml_dtypes
import numpy as np
from jax import lax
from jax.experimental import pallas as pl
from jax.experimental.pallas import tpu as pltpu
from jax.sharding import PartitionSpec as P

WIN = 8
L = 1500
HALF = L // 2
LPAD = 1536
KPAD = 768
FLO = 30
NB = 512
EVEN = NB // 2
SMOOTH = 4
LAGS = 256
SOURCES = 8
NEAR = 8
TILES = 8
LANES = 128
CORES = 2
X_CHIPS = 4

clip_level = 2.0
water_level = 0.1
epsilon = 1e-06

MESH = pl.DeviceIdType.MESH
VMEM_LIMIT = 48 * 1024 * 1024


def split(table):
    high = table.astype(np.float32).astype(ml_dtypes.bfloat16)
    low = (table - high.astype(np.float64)).astype(np.float32).astype(ml_dtypes.bfloat16)
    return high, low


def bin_order():
    return np.concatenate([np.arange(0, NB, 2), np.arange(1, NB, 2)])


@functools.lru_cache(maxsize=None)
def band_tables():
    sample = np.arange(HALF)
    out = np.zeros((2, 2, KPAD, NB), ml_dtypes.bfloat16)
    for parity in range(2):
        freq = FLO + np.arange(parity, NB, 2)
        phase = (sample[:, None] * freq[None, :] % L) * (2.0 * math.pi / L)
        table = np.concatenate([np.cos(phase), -np.sin(phase)], axis=1)
        out[parity, 0, :HALF], out[parity, 1, :HALF] = split(table)
    return out


@functools.lru_cache(maxsize=None)
def lag_tables():
    freq = FLO + bin_order()
    lag = np.arange(LAGS) - LAGS // 2
    phase = (freq[:, None] * lag[None, :] % L) * (2.0 * math.pi / L)
    table = np.concatenate([np.cos(phase), -np.sin(phase)], axis=0) / math.sqrt(WIN * NB)
    return np.stack(split(table))


@functools.lru_cache(maxsize=None)
def smooth_table():
    count = np.zeros((NB, NB))
    for centre in range(NB):
        for step in range(-SMOOTH, SMOOTH + 1):
            count[min(max(centre + step, 0), NB - 1), centre] += 1
    order = bin_order()
    return count[order][:, order].astype(ml_dtypes.bfloat16)


def dot(a, b):
    return jnp.dot(a, b, preferred_element_type=jnp.float32)


def halves(value):
    high = value.astype(jnp.bfloat16)
    return high, (value - high.astype(jnp.float32)).astype(jnp.bfloat16)


def dot3(value, high_table, low_table):
    high, low = halves(value)
    return dot(high, high_table) + dot(low, high_table) + dot(high, low_table)


def spectra_of(records, padded, band, smooth):
    centered = records - jnp.sum(records, axis=-1, keepdims=True) * (1.0 / L)
    power = jnp.sum(centered * centered, axis=-1, keepdims=True) * (1.0 / L)
    normed = jnp.clip(centered * (1.0 / jnp.sqrt(power + epsilon)), -clip_level, clip_level)
    padded[:, :L] = normed
    first = padded[:, :KPAD]
    second = pltpu.roll(padded[...], LPAD - HALF, 1)[:, :KPAD]
    even = dot3(first + second, band[0, 0], band[0, 1])
    odd = dot3(first - second, band[1, 0], band[1, 1])
    real = jnp.concatenate([even[:, :EVEN], odd[:, :EVEN]], axis=1)
    imag = jnp.concatenate([even[:, EVEN:], odd[:, EVEN:]], axis=1)
    amplitude = jnp.sqrt(real * real + imag * imag)
    high, low = halves(amplitude)
    smoothed = (dot(high, smooth[...]) + dot(low, smooth[...])) * (1.0 / (2 * SMOOTH + 1))
    mean = jnp.sum(amplitude, axis=-1, keepdims=True) * (water_level / NB)
    scale = 1.0 / (smoothed + mean + epsilon)
    return real * scale, imag * scale


def local_kernel(ids, records, band, smooth, spectra, kept, padded):
    base = (lax.axis_index("seg") * lax.axis_size("chan") + lax.axis_index("chan")) * records.shape[0]
    channels = records.shape[0]
    chunk = 16
    rows = chunk * WIN
    padded[:, LPAD - LANES :] = jnp.zeros((rows, LANES), jnp.float32)
    for start in range(0, channels, chunk):
        block = records[start : start + chunk].reshape(rows, L)
        real, imag = spectra_of(block, padded, band, smooth)
        spectra[start : start + chunk, :, :NB] = real.reshape(chunk, WIN, NB)
        spectra[start : start + chunk, :, NB:] = imag.reshape(chunk, WIN, NB)
    for s in range(SOURCES):
        local = ids[s] - base
        mine = jnp.logical_and(local >= 0, local < channels)
        row = spectra[jnp.clip(local, 0, channels - 1)]
        row = row * mine.astype(jnp.float32)
        for t in range(TILES):
            kept[s, t] = row[:, t * LANES : (t + 1) * LANES]


def exchange_kernel(dims, kept, spectra, sources, below, above, half, part, piece, r0, r1, r2, r3,
                    send, recv):
    xs, ys, zs = dims
    seg, chan = lax.axis_index("seg"), lax.axis_index("chan")
    z, core = seg // CORES, lax.rem(seg, CORES)
    y, x = chan // xs, lax.rem(chan, xs)
    per_core = SOURCES // CORES
    per_rank = per_core // xs
    per_y = TILES // ys
    channels = spectra.shape[0]
    total = lax.axis_size("seg") * lax.axis_size("chan")
    n_chan = lax.axis_size("chan")
    me = seg * n_chan + chan

    def at(z_, core_, y_, x_):
        return (z_ * CORES + core_, y_ * xs + x_)

    def of(index):
        return (index // n_chan, lax.rem(index, n_chan))

    sibling = at(z, 1 - core, y, x)
    x_peers = [(d, lax.rem(x + d, xs)) for d in range(1, xs)]
    y_peers = [(d, lax.rem(y + d, ys)) for d in range(1, ys)]
    z_peers = [(d, lax.rem(z + d, zs)) for d in range(1, zs)]
    after = of(lax.rem(me + 1, total))
    before = of(lax.rem(me + total - 1, total))

    barrier = pltpu.get_barrier_semaphore()
    greeted = [sibling, after, before]
    greeted += [at(z, core, y, p) for _, p in x_peers]
    greeted += [at(z, core, p, x) for _, p in y_peers]
    greeted += [at(p, core, y, x) for _, p in z_peers]
    for device in greeted:
        pl.semaphore_signal(barrier, inc=1, device_id=device, device_id_type=MESH)
    pl.semaphore_wait(barrier, len(greeted))

    slot = [0]

    def push(src, dst, device):
        k = slot[0]
        slot[0] += 1
        copy = pltpu.make_async_remote_copy(
            src_ref=src, dst_ref=dst, send_sem=send.at[k], recv_sem=recv.at[k],
            device_id=device, device_id_type=MESH)
        copy.start()
        return copy

    everything = []
    c0 = push(kept.at[pl.ds(per_core * (1 - core), per_core)], r0, sibling)
    up = push(spectra.at[pl.ds(channels - NEAR, NEAR)], below, after)
    down = push(spectra.at[pl.ds(0, NEAR)], above, before)
    c0.wait_recv()
    half[...] = kept[pl.ds(per_core * core, per_core)] + r0[...]
    c1 = [push(half.at[pl.ds(p * per_rank, per_rank)], r1.at[d - 1], at(z, core, y, p)) for d, p in x_peers]
    for c in c1:
        c.wait_recv()
    total_1 = half[pl.ds(x * per_rank, per_rank)]
    for d in range(xs - 1):
        total_1 += r1[d]
    part[...] = total_1
    c2 = [push(part.at[:, pl.ds(p * per_y, per_y)], r2.at[d - 1], at(z, core, p, x)) for d, p in y_peers]
    for c in c2:
        c.wait_recv()
    total_2 = part[:, pl.ds(y * per_y, per_y)]
    for d in range(ys - 1):
        total_2 += r2[d]
    piece[...] = total_2
    c3 = [push(piece, r3.at[d - 1], at(p, core, y, x)) for d, p in z_peers]
    for c in c3:
        c.wait_recv()
    for d in range(zs - 1):
        total_2 += r3[d]
    rank = (core * xs + x) * per_rank
    mine = sources.at[pl.ds(rank, per_rank), pl.ds(y * per_y, per_y)]
    mine[...] = total_2
    c4 = [push(mine, mine, at(z, core, p, x)) for d, p in y_peers]
    for c in c4:
        c.wait_recv()
    owned = sources.at[pl.ds(rank, per_rank)]
    c5 = [push(owned, owned, at(z, core, y, p)) for d, p in x_peers]
    c6 = [push(owned, owned, sibling)]
    for c, (d, _) in zip(c5, x_peers):
        c.wait_recv()
        origin = (core * xs + lax.rem(x + xs - d, xs)) * per_rank
        got = sources.at[pl.ds(origin, per_rank)]
        c6.append(push(got, got, sibling))
    for c in c6:
        c.wait_recv()
    up.wait_recv()
    down.wait_recv()
    for c in [c0, up, down] + c1 + c2 + c3 + c4 + c5 + c6:
        c.wait_send()


def result_kernel(pairs, count, sources, spectra, below, above, lags, source_out, pair_out,
                  near, by_window, cross, sems):
    channels = spectra.shape[0]
    base = (lax.axis_index("seg") * lax.axis_size("chan") + lax.axis_index("chan")) * channels
    copies = [
        pltpu.make_async_copy(below, near.at[pl.ds(0, NEAR)], sems.at[0]),
        pltpu.make_async_copy(spectra, near.at[pl.ds(NEAR, channels)], sems.at[1]),
        pltpu.make_async_copy(above, near.at[pl.ds(NEAR + channels, NEAR)], sems.at[2]),
    ] + [
        pltpu.make_async_copy(spectra.at[:, w], by_window.at[w], sems.at[3 + w]) for w in range(WIN)
    ]
    for c in copies:
        c.start()
    for c in copies:
        c.wait()
    slots = pair_out.shape[0]

    def one_pair(slot, carry):
        left = near[pairs[2 * slot] - base + NEAR]
        right = near[pairs[2 * slot + 1] - base + NEAR]
        l_re, l_im, r_re, r_im = left[:, :NB], left[:, NB:], right[:, :NB], right[:, NB:]
        cross[pl.ds(slot, 1), :NB] = jnp.sum(l_re * r_re + l_im * r_im, axis=0, keepdims=True)
        cross[pl.ds(slot, 1), NB:] = jnp.sum(l_re * r_im - l_im * r_re, axis=0, keepdims=True)
        return carry

    lax.fori_loop(0, slots, one_pair, 0, unroll=4)
    result = dot3(cross[:slots], lags[0], lags[1])
    live = lax.broadcasted_iota(jnp.int32, (slots, 1), 0) < count[0]
    pair_out[...] = result * live.astype(jnp.float32)

    half_tiles = TILES // 2

    def one_source(s, carry):
        for t in range(half_tiles):
            re = jnp.zeros((channels, LANES), jnp.float32)
            im = jnp.zeros((channels, LANES), jnp.float32)
            for w in range(WIN):
                s_re = sources[s, t, w : w + 1]
                s_im = sources[s, half_tiles + t, w : w + 1]
                c_re = by_window[w, :, t * LANES : (t + 1) * LANES]
                c_im = by_window[w, :, NB + t * LANES : NB + (t + 1) * LANES]
                re += s_re * c_re + s_im * c_im
                im += s_re * c_im - s_im * c_re
            cross[pl.ds(s * channels, channels), t * LANES : (t + 1) * LANES] = re
            cross[pl.ds(s * channels, channels), NB + t * LANES : NB + (t + 1) * LANES] = im
        return carry

    lax.fori_loop(0, SOURCES, one_source, 0)
    source_out[...] = dot3(cross[...], lags[0], lags[1])


def shards(dims, das_records, source_ids, near_pairs, pair_count):
    xs, ys, zs = dims
    channels = das_records.shape[0]
    vmem = pl.BlockSpec(memory_space=pltpu.VMEM)
    smem = pl.BlockSpec(memory_space=pltpu.SMEM)
    hbm = pl.BlockSpec(memory_space=pl.ANY)
    f32 = jnp.float32
    spectra, kept = pl.pallas_call(
        local_kernel,
        out_shape=(
            jax.ShapeDtypeStruct((channels, WIN, 2 * NB), f32),
            jax.ShapeDtypeStruct((SOURCES, TILES, WIN, LANES), f32),
        ),
        in_specs=[smem, vmem, vmem, vmem],
        out_specs=(vmem, vmem),
        scratch_shapes=[pltpu.VMEM((16 * WIN, LPAD), f32)],
        compiler_params=pltpu.CompilerParams(vmem_limit_bytes=VMEM_LIMIT),
        name="local_spectra",
    )(source_ids.reshape(-1), das_records, jnp.asarray(band_tables()), jnp.asarray(smooth_table()))
    per_core = SOURCES // CORES
    per_rank = per_core // xs
    per_y = TILES // ys
    n_copies = 3 + 2 * (xs - 1) + 2 * (ys - 1) + (zs - 1) + xs
    tile = (WIN, LANES)
    sources, below, above = pl.pallas_call(
        functools.partial(exchange_kernel, dims),
        out_shape=(
            jax.ShapeDtypeStruct((SOURCES, TILES) + tile, f32),
            jax.ShapeDtypeStruct((NEAR, WIN, 2 * NB), f32),
            jax.ShapeDtypeStruct((NEAR, WIN, 2 * NB), f32),
        ),
        in_specs=[vmem, hbm],
        out_specs=(vmem, hbm, hbm),
        scratch_shapes=[
            pltpu.VMEM((per_core, TILES) + tile, f32),
            pltpu.VMEM((per_rank, TILES) + tile, f32),
            pltpu.VMEM((per_rank, per_y) + tile, f32),
            pltpu.VMEM((per_core, TILES) + tile, f32),
            pltpu.VMEM((xs - 1, per_rank, TILES) + tile, f32),
            pltpu.VMEM((ys - 1, per_rank, per_y) + tile, f32),
            pltpu.VMEM((zs - 1, per_rank, per_y) + tile, f32),
            pltpu.SemaphoreType.DMA((n_copies,)),
            pltpu.SemaphoreType.DMA((n_copies,)),
        ],
        compiler_params=pltpu.CompilerParams(collective_id=0, has_side_effects=True),
        name="exchange",
    )(kept, spectra)
    source_xcorr, pair_xcorr = pl.pallas_call(
        result_kernel,
        out_shape=(
            jax.ShapeDtypeStruct((SOURCES * channels, LAGS), f32),
            jax.ShapeDtypeStruct((near_pairs.shape[0], LAGS), f32),
        ),
        in_specs=[smem, smem, vmem, hbm, hbm, hbm, vmem],
        out_specs=(vmem, vmem),
        scratch_shapes=[
            pltpu.VMEM((channels + 2 * NEAR, WIN, 2 * NB), f32),
            pltpu.VMEM((WIN, channels, 2 * NB), f32),
            pltpu.VMEM((SOURCES * channels, 2 * NB), f32),
            pltpu.SemaphoreType.DMA((3 + WIN,)),
        ],
        compiler_params=pltpu.CompilerParams(vmem_limit_bytes=VMEM_LIMIT),
        name="correlate",
    )(near_pairs.reshape(-1), pair_count, sources, spectra, below, above, jnp.asarray(lag_tables()))
    return source_xcorr.reshape(source_ids.shape + (channels, LAGS)), pair_xcorr


def solution(mesh, xs=X_CHIPS):
    dims = (xs, mesh.shape["chan"] // xs, mesh.shape["seg"] // CORES)
    in_specs = (P(("seg", "chan"), None, None), P(), P(("seg", "chan"), None), P(("seg", "chan")))
    out_specs = (P(None, None, ("seg", "chan"), None), P(("seg", "chan"), None))
    return jax.shard_map(
        functools.partial(shards, dims), mesh=mesh, in_specs=in_specs, out_specs=out_specs, check_vma=False
    )
```

time: 403 us -> 68.6 us (0.17)
  waiting for transfers between devices: 263 us -> 0 us
  Pallas kernels: 0 us -> 56.9 us
  between operations: 40.2 us -> 1.34 us
  matrix products: 31 us -> 0 us
  other arithmetic: 30.9 us -> 0 us
  local copies, waits for them, and re-layouts: 26.3 us -> 9.95 us
  starting transfers between devices: 10.6 us -> 0 us
    psum x1 -> x0, waiting for transfers between devices: 263 us -> none  [broadcast(): return lax.psum(kept, axis)]
    pallas_call x0 -> x3, Pallas kernels: none -> 56.9 us  [the longest x1 45.5 us: shards(): pl.pallas_call(functools.partial(exchange_kernel, dims), out_shape=(jax.S...]
    dot_general x7 -> x0, matrix products: 31 us -> none  [the longest x1 8.45 us: shards(): jnp.dot(normed, band_table(), precision=precise)]
    cos x2 -> x0, other arithmetic: 17.3 us -> none  [the longest x1 14 us: band_table(): return jnp.concatenate([jnp.cos(phases), -jnp.sin(phases)], axis=1)]
    ppermute x2 -> x0, starting transfers between devices: 10.6 us -> none  [passed_along(): return lax.ppermute(array, axis, pairs)]
    gather x2 -> x0, local copies, waits for them, and re-layouts: 7.43 us -> none  [the longest x1 4.67 us: shards(): jnp.take(extended, near_pairs[:, 1] - base_channel + ch_count, axis=0, mo...]
    reduce_sum x4 -> x0, other arithmetic: 6.21 us -> none  [the longest x1 5.49 us: correlate(): jnp.sum(left_real * right_real + left_imag * right_imag, axis=-2)]
    concatenate x2 -> x0, other arithmetic: 5.06 us -> none  [the longest x1 3.7 us: shards(): extended = jnp.concatenate([prev_spectra, spectra, next_spectra], axis=0)]
  transfers between devices with their start and end apart: 3 -> 0, of which waited for: 1 -> 0; matrix products, arithmetic and copies ran while one was open for 12% -> 0% of each run, Pallas kernels for 0% -> 0%
where the time goes in v1:
time: 68.6 us; the launch traced here: 68.2 us
  Pallas kernels  56.9 us (83%)
  local copies, waits for them, and re-layouts  9.95 us (15%)
  between operations  1.34 us (2%)
    pallas_call x1, Pallas kernels, shards(): pl.pallas_call(functools.partial(exchange_kernel, dims), out_shape=(jax.S...  45.5 us
    unnamed x20, local copies, waits for them, and re-layouts  9.73 us
    pallas_call x1, Pallas kernels, shards(): pl.pallas_call(result_kernel, out_shape=(jax.ShapeDtypeStruct((SOURCES *...  7.04 us
    pallas_call x1, Pallas kernels, shards(): pl.pallas_call(local_kernel, out_shape=(jax.ShapeDtypeStruct((channels, W...  4.35 us

profile of v1, /device:TPU:1, one launch (start us, length us, event | category | flops | bytes accessed | tf_op | source)
XLA Modules:
  0.0 68.2 jit_solution(5643603215515501255)
XLA Ops:
  1.3 0.8 %copy.11 = s32[4,2]{1,0:T(4,128)S(1)} copy(s32[4,2]{0,1:T(2,128)} %param.8) | data formatting | bytes 64 | tf_op args[1]
  2.0 0.1 reshape.14.ids
  2.1 0.8 %copy.10 = s32[128,2]{1,0:T(8,128)S(1)} copy(s32[128,2]{0,1:T(2,128)} %param.9) | data formatting | bytes 2048 | tf_op args[2]
  2.9 0.1 reshape.13.pairs
  3.1 0.0 copy-start.2
  3.1 1.4 %copy-done.2 = f32[32,8,1500]{2,1,0:T(8,128)S(1)} copy-done((f32[32,8,1500]{2,1,0:T(8,128)S(1)}, f32[32,8,1500]{2,1,0:T(8,128)}, u32[]{:S(2)}) %copy-start.2) | copy-done | bytes 1536024
  4.5 0.0 copy-start.4
  4.5 1.0 %copy-done.4 = bf16[512,512]{1,0:T(8,128)(2,1)S(1)} copy-done((bf16[512,512]{1,0:T(8,128)(2,1)S(1)}, bf16[512,512]{1,0:T(8,128)(2,1)}, u32[]{:S(2)}) %copy-start.4) | copy-done | bytes 524312
  5.5 0.0 copy-start.3
  5.5 4.4 %local_spectra.1 = (f32[32,8,1024]{2,1,0:T(8,128)S(1)}, f32[8,8,8,128]{3,2,1,0:T(8,128)S(1)}) custom-call(s32[8]{0:T(128)S(1)} %reshape.14.ids, f32[32,8,1500]{2,1,0:T(8,128)S(1)} %copy-done.2, bf16[2,2,768,512]{3,2,1,0:T(8,128)(2,1)} %constant.6.clone.band, bf16[512,512]{1,0:T(8,128)(2,1)S(1)} %copy-done.4), custom_call_target="tpu_custom_call" | custom-call | tf_op jit(solution)/shard_map/local_spectra/pallas_call | solution.py:284
  9.9 0.0 copy-start
  9.9 1.0 %copy-done = f32[32,8,1024]{2,1,0:T(8,128)} copy-done((f32[32,8,1024]{2,1,0:T(8,128)}, f32[32,8,1024]{2,1,0:T(8,128)S(1)}, u32[]{:S(2)}) %copy-start) | copy-done | bytes 1048600
  10.8 0.0 copy-start.8
  10.8 0.7 %copy-done.8 = f32[8,8,8,128]{3,2,1,0:T(8,128)} copy-done((f32[8,8,8,128]{3,2,1,0:T(8,128)}, f32[8,8,8,128]{3,2,1,0:T(8,128)S(1)}, u32[]{:S(2)}) %copy-start.8) | copy-done | bytes 262168
  11.5 45.5 %exchange.1 = (f32[8,8,8,128]{3,2,1,0:T(8,128)}, f32[8,8,1024]{2,1,0:T(8,128)}, f32[8,8,1024]{2,1,0:T(8,128)}) custom-call(f32[8,8,8,128]{3,2,1,0:T(8,128)} %copy-done.8, f32[32,8,1024]{2,1,0:T(8,128)} %copy-done), custom_call_target="tpu_custom_call" | custom-call | tf_op jit(solution)/shard_map/exchange/pallas_call | solution.py:301
  57.0 0.0 copy-done.3
  57.1 0.0 copy-start.1
  57.1 1.2 %copy-done.1 = f32[32,8,1024]{2,1,0:T(8,128)S(1)} copy-done((f32[32,8,1024]{2,1,0:T(8,128)S(1)}, f32[32,8,1024]{2,1,0:T(8,128)}, u32[]{:S(2)}) %copy-start.1) | copy-done | bytes 1048600
  58.3 0.0 copy-start.5
  58.3 0.9 %copy-done.5 = f32[8,8,8,128]{3,2,1,0:T(8,128)S(1)} copy-done((f32[8,8,8,128]{3,2,1,0:T(8,128)S(1)}, f32[8,8,8,128]{3,2,1,0:T(8,128)}, u32[]{:S(2)}) %copy-start.5) | copy-done | bytes 262168
  59.2 0.0 copy-start.6
  59.2 0.9 %copy-done.6 = f32[8,8,1024]{2,1,0:T(8,128)S(1)} copy-done((f32[8,8,1024]{2,1,0:T(8,128)S(1)}, f32[8,8,1024]{2,1,0:T(8,128)}, u32[]{:S(2)}) %copy-start.6) | copy-done | bytes 262168
  60.2 0.0 copy-start.7
  60.2 0.9 %copy-done.7 = f32[8,8,1024]{2,1,0:T(8,128)S(1)} copy-done((f32[8,8,1024]{2,1,0:T(8,128)S(1)}, f32[8,8,1024]{2,1,0:T(8,128)}, u32[]{:S(2)}) %copy-start.7) | copy-done | bytes 262168
  61.1 7.0 %correlate.1 = (f32[256,256]{1,0:T(8,128)}, f32[128,256]{1,0:T(8,128)}) custom-call(s32[256]{0:T(256)S(1)} %reshape.13.pairs, s32[1]{0:T(128)S(6)} %copy.12.count, f32[8,8,8,128]{3,2,1,0:T(8,128)S(1)} %copy-done.5, f32[32,8,1024]{2,1,0:T(8,128)S(1)} %copy-done.1, f32[8,8,1024]{2,1,0:T(8,128)S(1)} %copy-done.6, f32[8,8,1024]{2,1,0:T(8,128)S(1)} %copy-done.7, ...), custom_call_target="tpu_custom_call" | custom-call | tf_op jit(solution)/shard_map/correlate/pallas_call | solution.py:324
Async XLA Ops:
  3.1 1.4 %copy-start.2 = (f32[32,8,1500]{2,1,0:T(8,128)S(1)}, f32[32,8,1500]{2,1,0:T(8,128)}, u32[]{:S(2)}) copy-start(f32[32,8,1500]{2,1,0:T(8,128)} %records.1) | copy-start | bytes 4608004
  4.5 1.0 %copy-start.4 = (bf16[512,512]{1,0:T(8,128)(2,1)S(1)}, bf16[512,512]{1,0:T(8,128)(2,1)}, u32[]{:S(2)}) copy-start(bf16[512,512]{1,0:T(8,128)(2,1)} %constant.7.clone.smooth) | copy-start | bytes 1572868
  5.5 51.5 %copy-start.3 = (bf16[2,1024,256]{2,1,0:T(8,128)(2,1)S(1)}, bf16[2,1024,256]{2,1,0:T(8,128)(2,1)}, u32[]{:S(2)}) copy-start(bf16[2,1024,256]{2,1,0:T(8,128)(2,1)} %constant.8.clone.lags) | copy-start | bytes 3145732
  9.9 1.0 %copy-start = (f32[32,8,1024]{2,1,0:T(8,128)}, f32[32,8,1024]{2,1,0:T(8,128)S(1)}, u32[]{:S(2)}) copy-start(f32[32,8,1024]{2,1,0:T(8,128)S(1)} %get-tuple-element.10.spectra) | copy-start | bytes 3145732
  10.8 0.7 %copy-start.8 = (f32[8,8,8,128]{3,2,1,0:T(8,128)}, f32[8,8,8,128]{3,2,1,0:T(8,128)S(1)}, u32[]{:S(2)}) copy-start(f32[8,8,8,128]{3,2,1,0:T(8,128)S(1)} %get-tuple-element.9.kept) | copy-start | bytes 786436
  57.1 1.2 %copy-start.1 = (f32[32,8,1024]{2,1,0:T(8,128)S(1)}, f32[32,8,1024]{2,1,0:T(8,128)}, u32[]{:S(2)}) copy-start(f32[32,8,1024]{2,1,0:T(8,128)} %copy-done) | copy-start | bytes 3145732
  58.3 0.9 %copy-start.5 = (f32[8,8,8,128]{3,2,1,0:T(8,128)S(1)}, f32[8,8,8,128]{3,2,1,0:T(8,128)}, u32[]{:S(2)}) copy-start(f32[8,8,8,128]{3,2,1,0:T(8,128)} %get-tuple-element.11.sources) | copy-start | bytes 786436
  59.2 0.9 %copy-start.6 = (f32[8,8,1024]{2,1,0:T(8,128)S(1)}, f32[8,8,1024]{2,1,0:T(8,128)}, u32[]{:S(2)}) copy-start(f32[8,8,1024]{2,1,0:T(8,128)} %get-tuple-element.12.below) | copy-start | bytes 786436
  60.2 0.9 %copy-start.7 = (f32[8,8,1024]{2,1,0:T(8,128)S(1)}, f32[8,8,1024]{2,1,0:T(8,128)}, u32[]{:S(2)}) copy-start(f32[8,8,1024]{2,1,0:T(8,128)} %get-tuple-element.13.above) | copy-start | bytes 786436

commit v2 on v1

v2 whole, which is shorter than its diff:
```python
import functools
import math

import jax
import jax.numpy as jnp
import ml_dtypes
import numpy as np
from jax import lax
from jax.experimental import pallas as pl
from jax.experimental.pallas import tpu as pltpu
from jax.sharding import PartitionSpec as P

WIN = 8
L = 1500
HALF = L // 2
LPAD = 1536
KPAD = 768
FLO = 30
NB = 512
EVEN = NB // 2
SMOOTH = 4
LAGS = 256
SOURCES = 8
NEAR = 8
ROWS = 8
LANES = 128
CORES = 2
X_CHIPS = 4

clip_level = 2.0
water_level = 0.1
epsilon = 1e-06

SMOOTH_AT = 4 * KPAD
LAG_AT = SMOOTH_AT + NB
TABLE_ROWS = LAG_AT + 2 * NB

MESH = pl.DeviceIdType.MESH
VMEM_LIMIT = 62 * 1024 * 1024


def split(table):
    high = table.astype(np.float32).astype(ml_dtypes.bfloat16)
    low = (table - high.astype(np.float64)).astype(np.float32).astype(ml_dtypes.bfloat16)
    return high, low


def bin_order():
    return np.concatenate([np.arange(0, NB, 2), np.arange(1, NB, 2)])


@functools.lru_cache(maxsize=None)
def band_tables():
    sample = np.arange(HALF)
    out = np.zeros((2, 2, KPAD, NB), ml_dtypes.bfloat16)
    for parity in range(2):
        freq = FLO + np.arange(parity, NB, 2)
        phase = (sample[:, None] * freq[None, :] % L) * (2.0 * math.pi / L)
        table = np.concatenate([np.cos(phase), -np.sin(phase)], axis=1)
        out[parity, 0, :HALF], out[parity, 1, :HALF] = split(table)
    return out


@functools.lru_cache(maxsize=None)
def lag_tables():
    freq = FLO + bin_order()
    lag = np.arange(LAGS) - LAGS // 2
    phase = (freq[:, None] * lag[None, :] % L) * (2.0 * math.pi / L)
    table = np.concatenate([np.cos(phase), -np.sin(phase)], axis=0) / math.sqrt(WIN * NB)
    return np.stack(split(table))


@functools.lru_cache(maxsize=None)
def smooth_table():
    count = np.zeros((NB, NB))
    for centre in range(NB):
        for step in range(-SMOOTH, SMOOTH + 1):
            count[min(max(centre + step, 0), NB - 1), centre] += 1
    order = bin_order()
    return count[order][:, order].astype(ml_dtypes.bfloat16)


def all_tables():
    band = band_tables().reshape(SMOOTH_AT, NB)
    lags = np.concatenate(list(lag_tables()), axis=1)
    return np.concatenate([band, smooth_table(), lags], axis=0)


def dot(a, b):
    return jnp.dot(a, b, preferred_element_type=jnp.float32)


def halves(value):
    high = value.astype(jnp.bfloat16)
    return high, (value - high.astype(jnp.float32)).astype(jnp.bfloat16)


def dot3(value, high_table, low_table):
    high, low = halves(value)
    return dot(high, high_table) + dot(low, high_table) + dot(high, low_table)


def spectra_of(records, padded, tables):
    centered = records - jnp.sum(records, axis=-1, keepdims=True) * (1.0 / L)
    power = jnp.sum(centered * centered, axis=-1, keepdims=True) * (1.0 / L)
    normed = jnp.clip(centered * (1.0 / jnp.sqrt(power + epsilon)), -clip_level, clip_level)
    padded[:, :L] = normed
    first = padded[:, :KPAD]
    second = pltpu.roll(padded[...], LPAD - HALF, 1)[:, :KPAD]
    even = dot3(first + second, tables[:KPAD], tables[KPAD : 2 * KPAD])
    odd = dot3(first - second, tables[2 * KPAD : 3 * KPAD], tables[3 * KPAD : SMOOTH_AT])
    real = jnp.concatenate([even[:, :EVEN], odd[:, :EVEN]], axis=1)
    imag = jnp.concatenate([even[:, EVEN:], odd[:, EVEN:]], axis=1)
    amplitude = jnp.sqrt(real * real + imag * imag)
    high, low = halves(amplitude)
    smooth = tables[SMOOTH_AT:LAG_AT]
    smoothed = (dot(high, smooth) + dot(low, smooth)) * (1.0 / (2 * SMOOTH + 1))
    mean = jnp.sum(amplitude, axis=-1, keepdims=True) * (water_level / NB)
    scale = 1.0 / (smoothed + mean + epsilon)
    return real * scale, imag * scale


def kernel(dims, ids, pairs, count, records_hbm, tables_hbm, source_out, pair_out,
           records, tables, padded, near, by_window, kept, half, r0, ra1, rb1, ra2, rb2,
           piece, r3, sources, acc, pair_cross, source_res, pair_res, load, send, recv):
    xs, ys, zs = dims
    seg, chan = lax.axis_index("seg"), lax.axis_index("chan")
    n_chan = lax.axis_size("chan")
    total = lax.axis_size("seg") * n_chan
    me = seg * n_chan + chan
    z, core = seg // CORES, lax.rem(seg, CORES)
    y, x = chan // xs, lax.rem(chan, xs)
    channels = records.shape[0]
    base = me * channels
    per_core = SOURCES // CORES
    group = per_core // 2
    span = WIN // ys

    loads = [pltpu.make_async_copy(records_hbm, records, load.at[0])] + [
        pltpu.make_async_copy(tables_hbm.at[lo:hi], tables.at[lo:hi], load.at[1 + k])
        for k, (lo, hi) in enumerate([(0, SMOOTH_AT), (SMOOTH_AT, LAG_AT), (LAG_AT, TABLE_ROWS)])
    ]
    for c in loads:
        c.start()

    def at(z_, core_, y_, x_):
        return (z_ * CORES + core_, y_ * xs + x_)

    def of(index):
        return (index // n_chan, lax.rem(index, n_chan))

    def at_x(d):
        return at(z, core, y, lax.rem(x + d, xs))

    def at_y(d):
        return at(z, core, lax.rem(y + d, ys), x)

    def at_z(d):
        return at(lax.rem(z + d, zs), core, y, x)

    sibling = at(z, 1 - core, y, x)
    after = of(lax.rem(me + 1, total))
    before = of(lax.rem(me + total - 1, total))

    barrier = pltpu.get_barrier_semaphore()
    greeted = [sibling, after, before]
    greeted += [at_x(d) for d in range(1, xs)]
    greeted += [at_y(d) for d in range(1, ys)]
    greeted += [at_z(d) for d in range(1, zs)]
    for device in greeted:
        pl.semaphore_signal(barrier, inc=1, device_id=device, device_id_type=MESH)

    tail = padded.shape[0]
    padded[:, LPAD - LANES :] = jnp.zeros((tail, LANES), jnp.float32)
    acc[...] = jnp.zeros_like(acc)

    loads[0].wait()
    rows = [records[jnp.clip(ids[s % 2, s // 2] - base, 0, channels - 1)] for s in range(SOURCES)]
    block = jnp.concatenate(rows, axis=0)
    loads[1].wait()
    loads[2].wait()
    real, imag = spectra_of(block, padded.at[pl.ds(0, SOURCES * WIN)], tables)
    for s in range(SOURCES):
        local = ids[s % 2, s // 2] - base
        mine = jnp.logical_and(local >= 0, local < channels).astype(jnp.float32)
        for r in range(ROWS):
            part = real if r < ROWS // 2 else imag
            lane = (r % (ROWS // 2)) * LANES
            kept[s, :, r, :] = part[s * WIN : (s + 1) * WIN, lane : lane + LANES] * mine

    used = [0]

    def slots(number):
        first = used[0]
        used[0] += number
        return first

    def remote(k, src, dst, device):
        return pltpu.make_async_remote_copy(
            src_ref=src, dst_ref=dst, send_sem=send.at[k], recv_sem=recv.at[k],
            device_id=device, device_id_type=MESH)

    def start(copies):
        for c in copies:
            c.start()
        return copies

    def arrive(copies):
        for c in copies:
            c.wait_recv()

    def spectra_to_near(places):
        block = jnp.concatenate([records[lo:hi] for lo, hi in places], axis=0)
        real, imag = spectra_of(block.reshape(-1, L), padded, tables)
        row = 0
        for lo, hi in places:
            size = hi - lo
            near[NEAR + lo : NEAR + hi, :, :NB] = real[row * WIN : (row + size) * WIN].reshape(size, WIN, NB)
            near[NEAR + lo : NEAR + hi, :, NB:] = imag[row * WIN : (row + size) * WIN].reshape(size, WIN, NB)
            row += size

    pl.semaphore_wait(barrier, len(greeted))
    k = slots(1)
    core_copy = start([remote(k, kept.at[pl.ds(per_core * (1 - core), per_core)], r0, sibling)])
    arrive(core_copy)
    half[...] = kept[pl.ds(per_core * core, per_core)] + r0[...]

    def to(d, mine, n):
        return pl.ds(lax.rem(mine + d, n) * span, span)

    ka, kb = slots(ys), slots(zs)
    first = start(
        [remote(ka + d, half.at[pl.ds(0, group), to(d, y, ys)], ra1.at[d - 1], at_y(d)) for d in range(1, ys)]
        + [remote(kb + d, half.at[pl.ds(group, group), to(d, z, zs)], rb1.at[d - 1], at_z(d)) for d in range(1, zs)])

    spectra_to_near([(0, NEAR), (channels - NEAR, channels)])
    k = slots(2)
    halo = start([
        remote(k, near.at[pl.ds(channels, NEAR)], near.at[pl.ds(0, NEAR)], after),
        remote(k + 1, near.at[pl.ds(NEAR, NEAR)], near.at[pl.ds(NEAR + channels, NEAR)], before)])
    spectra_to_near([(NEAR, channels - NEAR)])
    turned = [
        pltpu.make_async_copy(near.at[pl.ds(NEAR, channels), w], by_window.at[w], load.at[len(loads) + w])
        for w in range(WIN)
    ]
    for c in turned:
        c.start()

    arrive(first)
    piece[0] = half[:group, pl.ds(y * span, span)] + sum(ra1[d] for d in range(ys - 1))
    piece[1] = half[group:, pl.ds(z * span, span)] + sum(rb1[d] for d in range(zs - 1))
    ka, kb = slots(zs), slots(ys)
    second = start(
        [remote(ka + d, piece.at[0], ra2.at[d - 1], at_z(d)) for d in range(1, zs)]
        + [remote(kb + d, piece.at[1], rb2.at[d - 1], at_y(d)) for d in range(1, ys)])
    arrive(second)
    piece[2] = piece[0] + sum(ra2[d] for d in range(zs - 1))
    piece[3] = piece[1] + sum(rb2[d] for d in range(ys - 1))
    k = slots(xs)
    third = start([remote(k + d, piece.at[pl.ds(2, 2)], r3.at[d - 1], at_x(d)) for d in range(1, xs)])

    arrive(halo)
    slot_count = pair_cross.shape[0]

    def one_pair(slot, carry):
        left = near[jnp.clip(pairs[0, slot] - base + NEAR, 0, channels + 2 * NEAR - 1)]
        right = near[jnp.clip(pairs[1, slot] - base + NEAR, 0, channels + 2 * NEAR - 1)]
        l_re, l_im, r_re, r_im = left[:, :NB], left[:, NB:], right[:, :NB], right[:, NB:]
        pair_cross[pl.ds(slot, 1), :NB] = jnp.sum(l_re * r_re + l_im * r_im, axis=0, keepdims=True)
        pair_cross[pl.ds(slot, 1), NB:] = jnp.sum(l_re * r_im - l_im * r_re, axis=0, keepdims=True)
        return carry

    lax.fori_loop(0, slot_count, one_pair, 0, unroll=4)

    arrive(third)
    whole = piece[2:] + sum(r3[d] for d in range(xs - 1))
    own = core * per_core
    other = (1 - core) * per_core
    sources[pl.ds(own, group), pl.ds(y * span, span)] = whole[0]
    sources[pl.ds(own + group, group), pl.ds(z * span, span)] = whole[1]

    def block_a(owner, origin):
        return sources.at[pl.ds(owner, group), pl.ds(origin * span, span)]

    def block_b(owner, origin):
        return sources.at[pl.ds(owner + group, group), pl.ds(origin * span, span)]

    ka, kb, fa, fb = slots(ys), slots(zs), slots(ys), slots(zs)

    def gather_a(d):
        return remote(ka + d, block_a(own, y), block_a(own, y), at_y(d))

    def gather_b(d):
        return remote(kb + d, block_b(own, z), block_b(own, z), at_z(d))

    def pass_a(d):
        got = block_a(own, lax.rem(y + ys - d, ys))
        return remote(fa + d, got, got, sibling)

    def pass_b(d):
        got = block_b(own, lax.rem(z + zs - d, zs))
        return remote(fb + d, got, got, sibling)

    fourth = start([g(d) for d in range(1, ys) for g in (gather_a, gather_b)])
    start([pass_a(0), pass_b(0)])

    for c in loads[3:] + turned:
        c.wait()
    result = dot3(pair_cross[...], tables[LAG_AT:, :LAGS], tables[LAG_AT:, LAGS:])
    live = lax.broadcasted_iota(jnp.int32, (slot_count, 1), 0) < count[0]
    pair_res[...] = result * live.astype(jnp.float32)
    pair_store = pltpu.make_async_copy(pair_res, pair_out, load.at[0])
    pair_store.start()

    def add_window(s, w):
        for t in range(ROWS // 2):
            s_re = sources[s, w, t : t + 1]
            s_im = sources[s, w, ROWS // 2 + t : ROWS // 2 + t + 1]
            re, im = slice(t * LANES, (t + 1) * LANES), slice(NB + t * LANES, NB + (t + 1) * LANES)
            c_re = by_window[w, :, re]
            c_im = by_window[w, :, im]
            acc[s, :, re] += s_re * c_re + s_im * c_im
            acc[s, :, im] += s_re * c_im - s_im * c_re

    def add_blocks(owner, d):
        for g in range(group):
            for v in range(span):
                add_window(owner + g, lax.rem(y + ys - d, ys) * span + v)
                add_window(owner + group + g, lax.rem(z + zs - d, zs) * span + v)

    def nth(i):
        return jnp.where(lax.rem(i, 2) == 1, (i + 1) // 2, lax.rem(ys - i // 2, ys))

    add_blocks(own, 0)

    def step(i, carry):
        d, previous = nth(i), nth(i - 1)
        gather_a(d).wait_recv()
        pass_a(d).start()
        gather_b(d).wait_recv()
        pass_b(d).start()
        add_blocks(own, d)
        pass_a(previous).wait_recv()
        pass_b(previous).wait_recv()
        add_blocks(other, previous)
        return carry

    lax.fori_loop(1, ys, step, 0)
    source_res[0] = dot3(acc[pl.ds(own, per_core)].reshape(per_core * channels, 2 * NB), tables[LAG_AT:, :LAGS], tables[LAG_AT:, LAGS:])
    store_own = pltpu.make_async_copy(source_res.at[0], source_out.at[own // per_core], load.at[1])
    store_own.start()
    last = ys // 2
    pass_a(last).wait_recv()
    pass_b(last).wait_recv()
    add_blocks(other, last)
    source_res[1] = dot3(acc[pl.ds(other, per_core)].reshape(per_core * channels, 2 * NB), tables[LAG_AT:, :LAGS], tables[LAG_AT:, LAGS:])
    store_other = pltpu.make_async_copy(source_res.at[1], source_out.at[other // per_core], load.at[2])
    store_other.start()
    for c in core_copy + first + halo + second + third + fourth + [p(d) for d in range(ys) for p in (pass_a, pass_b)]:
        c.wait_send()
    pair_store.wait()
    store_own.wait()
    store_other.wait()


def shards(dims, das_records, source_ids, near_pairs, pair_count):
    xs, ys, zs = dims
    channels = das_records.shape[0]
    slot_count = near_pairs.shape[0]
    smem = pl.BlockSpec(memory_space=pltpu.SMEM)
    hbm = pl.BlockSpec(memory_space=pl.ANY)
    f32 = jnp.float32
    per_core = SOURCES // CORES
    group = per_core // 2
    span = WIN // ys
    tables = all_tables()
    tile = (ROWS, LANES)
    block = (group, span) + tile
    n_copies = 3 + 4 * ys + 4 * zs + xs
    source_xcorr, pair_xcorr = pl.pallas_call(
        functools.partial(kernel, dims),
        out_shape=(
            jax.ShapeDtypeStruct((CORES, per_core * channels, LAGS), f32),
            jax.ShapeDtypeStruct((slot_count, LAGS), f32),
        ),
        in_specs=[smem, smem, smem, hbm, hbm],
        out_specs=(hbm, hbm),
        scratch_shapes=[
            pltpu.VMEM(das_records.shape, f32),
            pltpu.VMEM(tables.shape, jnp.bfloat16),
            pltpu.VMEM((2 * NEAR * WIN, LPAD), f32),
            pltpu.VMEM((channels + 2 * NEAR, WIN, 2 * NB), f32),
            pltpu.VMEM((WIN, channels, 2 * NB), f32),
            pltpu.VMEM((SOURCES, WIN) + tile, f32),
            pltpu.VMEM((per_core, WIN) + tile, f32),
            pltpu.VMEM((per_core, WIN) + tile, f32),
            pltpu.VMEM((ys - 1,) + block, f32),
            pltpu.VMEM((zs - 1,) + block, f32),
            pltpu.VMEM((zs - 1,) + block, f32),
            pltpu.VMEM((ys - 1,) + block, f32),
            pltpu.VMEM((4,) + block, f32),
            pltpu.VMEM((xs - 1, 2) + block, f32),
            pltpu.VMEM((SOURCES, WIN) + tile, f32),
            pltpu.VMEM((SOURCES, channels, 2 * NB), f32),
            pltpu.VMEM((slot_count, 2 * NB), f32),
            pltpu.VMEM((CORES, per_core * channels, LAGS), f32),
            pltpu.VMEM((slot_count, LAGS), f32),
            pltpu.SemaphoreType.DMA((4 + WIN,)),
            pltpu.SemaphoreType.DMA((n_copies,)),
            pltpu.SemaphoreType.DMA((n_copies,)),
        ],
        compiler_params=pltpu.CompilerParams(
            collective_id=0, has_side_effects=True, vmem_limit_bytes=VMEM_LIMIT),
        name="correlate_all",
    )(source_ids.T, near_pairs.T, pair_count, das_records, jnp.asarray(tables))
    return source_xcorr.reshape(source_ids.shape + (channels, LAGS)), pair_xcorr


def solution(mesh, xs=X_CHIPS):
    dims = (xs, mesh.shape["chan"] // xs, mesh.shape["seg"] // CORES)
    in_specs = (P(("seg", "chan"), None, None), P(), P(("seg", "chan"), None), P(("seg", "chan")))
    out_specs = (P(None, None, ("seg", "chan"), None), P(("seg", "chan"), None))
    return jax.shard_map(
        functools.partial(shards, dims), mesh=mesh, in_specs=in_specs, out_specs=out_specs, check_vma=False
    )
```

time: 68.6 us -> 49.7 us (0.72)
  Pallas kernels: 56.9 us -> 45 us
  local copies, waits for them, and re-layouts: 9.95 us -> 3.24 us
    pallas_call x3 -> x1, Pallas kernels: 56.9 us -> 45 us  [shards(): pl.pallas_call(functools.partial(kernel, dims), out_shape=(jax.ShapeDtype...]
    unnamed x20 -> x2, local copies, waits for them, and re-layouts: 9.73 us -> 3.24 us
where the time goes in v2:
time: 49.7 us; the launch traced here: 49.5 us
  Pallas kernels  45 us (91%)
  local copies, waits for them, and re-layouts  3.24 us (7%)
  between operations  1.29 us (3%)
    pallas_call x1, Pallas kernels, shards(): pl.pallas_call(functools.partial(kernel, dims), out_shape=(jax.ShapeDtype...  45 us
    unnamed x2, local copies, waits for them, and re-layouts  3.24 us

profile of v2, /device:TPU:1, one launch (start us, length us, event | category | flops | bytes accessed | tf_op | source)
XLA Modules:
  0.0 49.5 jit_solution(12269055081254201405)
XLA Ops:
  1.3 45.0 %correlate_all.1 = (f32[2,128,256]{2,1,0:T(8,128)}, f32[128,256]{1,0:T(8,128)}) custom-call(s32[2,4]{1,0:T(2,128)} %bitcast.4, s32[2,128]{1,0:T(2,128)} %bitcast.5, s32[1]{0:T(128)S(6)} %copy.9.count, f32[32,8,1500]{2,1,0:T(8,128)} %records_hbm.1, bf16[4608,512]{1,0:T(8,128)(2,1)} %constant.2.clone.tables_hbm), custom_call_target="tpu_custom_call" | custom-call | tf_op jit(solution)/shard_map/correlate_all/pallas_call | solution.py:380
  46.3 1.7 %copy.10 = f32[4,2,32,256]{3,2,1,0:T(8,128)} copy(f32[4,2,32,256]{3,2,1,0:T(8,128)} %bitcast.3) | data formatting | bytes 524288
  47.9 1.6 %copy.11 = f32[128,256]{1,0:T(8,128)} copy(f32[128,256]{1,0:T(8,128)} %get-tuple-element.9) | data formatting | bytes 262144

commit v3 on v2

--- a/solution.py
+++ b/solution.py
@@ -26,6 +26,7 @@
 LANES = 128
 CORES = 2
 X_CHIPS = 4
+PARTS = 2
 
 clip_level = 2.0
 water_level = 0.1
@@ -97,14 +98,19 @@
 
 def dot3(value, high_table, low_table):
     high, low = halves(value)
-    return dot(high, high_table) + dot(low, high_table) + dot(high, low_table)
-
-
-def spectra_of(records, padded, tables):
+    rows = value.shape[0]
+    both = dot(jnp.concatenate([high, low], axis=0), high_table)
+    return both[:rows] + both[rows:] + dot(high, low_table)
+
+
+def normalize_into(records, padded):
     centered = records - jnp.sum(records, axis=-1, keepdims=True) * (1.0 / L)
     power = jnp.sum(centered * centered, axis=-1, keepdims=True) * (1.0 / L)
     normed = jnp.clip(centered * (1.0 / jnp.sqrt(power + epsilon)), -clip_level, clip_level)
     padded[:, :L] = normed
+
+
+def spectra_of(padded, tables):
     first = padded[:, :KPAD]
     second = pltpu.roll(padded[...], LPAD - HALF, 1)[:, :KPAD]
     even = dot3(first + second, tables[:KPAD], tables[KPAD : 2 * KPAD])
@@ -114,15 +120,21 @@
     amplitude = jnp.sqrt(real * real + imag * imag)
     high, low = halves(amplitude)
     smooth = tables[SMOOTH_AT:LAG_AT]
-    smoothed = (dot(high, smooth) + dot(low, smooth)) * (1.0 / (2 * SMOOTH + 1))
+    rows = amplitude.shape[0]
+    both = dot(jnp.concatenate([high, low], axis=0), smooth)
+    smoothed = (both[:rows] + both[rows:]) * (1.0 / (2 * SMOOTH + 1))
     mean = jnp.sum(amplitude, axis=-1, keepdims=True) * (water_level / NB)
     scale = 1.0 / (smoothed + mean + epsilon)
     return real * scale, imag * scale
 
 
-def kernel(dims, ids, pairs, count, records_hbm, tables_hbm, source_out, pair_out,
+def far_first(n):
+    return sorted(range(1, n), key=lambda d: -min(d, n - d))
+
+
+def kernel(dims, ids_hbm, pairs_hbm, count_hbm, records_hbm, tables_hbm, source_out, pair_out,
            records, tables, padded, near, by_window, kept, half, r0, ra1, rb1, ra2, rb2,
-           piece, r3, sources, acc, pair_cross, source_res, pair_res, load, send, recv):
+           piece, r3, sources, acc, pair_cross, source_res, pair_res, ids, pairs, count, load, send, recv):
     xs, ys, zs = dims
     seg, chan = lax.axis_index("seg"), lax.axis_index("chan")
     n_chan = lax.axis_size("chan")
@@ -136,50 +148,57 @@
     group = per_core // 2
     span = WIN // ys
 
+    def at(z_, core_, y_, x_):
+        return (z_ * CORES + core_, y_ * xs + x_)
+
+    def of(index):
+        return (index // n_chan, lax.rem(index, n_chan))
+
+    def at_x(d):
+        return at(z, core, y, lax.rem(x + d, xs))
+
+    def at_y(d):
+        return at(z, core, lax.rem(y + d, ys), x)
+
+    def at_z(d):
+        return at(lax.rem(z + d, zs), core, y, x)
+
+    sibling = at(z, 1 - core, y, x)
+    after = of(lax.rem(me + 1, total))
+    before = of(lax.rem(me + total - 1, total))
+
+    barrier = pltpu.get_barrier_semaphore()
+    y_far, x_far = far_first(ys), far_first(xs)
+    greeted = [there(d) for d in y_far for there in (at_y, at_z)]
+    greeted += [at_x(d) for d in x_far] + [after, before, sibling]
+    for device in greeted:
+        pl.semaphore_signal(barrier, inc=1, device_id=device, device_id_type=MESH)
+
+    numbers = [
+        pltpu.make_async_copy(src, dst, load.at[4 + k])
+        for k, (src, dst) in enumerate([(ids_hbm, ids), (pairs_hbm, pairs), (count_hbm, count)])
+    ]
+    numbers[0].start()
     loads = [pltpu.make_async_copy(records_hbm, records, load.at[0])] + [
         pltpu.make_async_copy(tables_hbm.at[lo:hi], tables.at[lo:hi], load.at[1 + k])
         for k, (lo, hi) in enumerate([(0, SMOOTH_AT), (SMOOTH_AT, LAG_AT), (LAG_AT, TABLE_ROWS)])
     ]
-    for c in loads:
+    for c in loads[:3] + numbers[1:]:
         c.start()
-
-    def at(z_, core_, y_, x_):
-        return (z_ * CORES + core_, y_ * xs + x_)
-
-    def of(index):
-        return (index // n_chan, lax.rem(index, n_chan))
-
-    def at_x(d):
-        return at(z, core, y, lax.rem(x + d, xs))
-
-    def at_y(d):
-        return at(z, core, lax.rem(y + d, ys), x)
-
-    def at_z(d):
-        return at(lax.rem(z + d, zs), core, y, x)
-
-    sibling = at(z, 1 - core, y, x)
-    after = of(lax.rem(me + 1, total))
-    before = of(lax.rem(me + total - 1, total))
-
-    barrier = pltpu.get_barrier_semaphore()
-    greeted = [sibling, after, before]
-    greeted += [at_x(d) for d in range(1, xs)]
-    greeted += [at_y(d) for d in range(1, ys)]
-    greeted += [at_z(d) for d in range(1, zs)]
-    for device in greeted:
-        pl.semaphore_signal(barrier, inc=1, device_id=device, device_id_type=MESH)
 
     tail = padded.shape[0]
     padded[:, LPAD - LANES :] = jnp.zeros((tail, LANES), jnp.float32)
     acc[...] = jnp.zeros_like(acc)
 
+    numbers[0].wait()
     loads[0].wait()
     rows = [records[jnp.clip(ids[s % 2, s // 2] - base, 0, channels - 1)] for s in range(SOURCES)]
     block = jnp.concatenate(rows, axis=0)
+    owned = padded.at[pl.ds(0, SOURCES * WIN)]
+    normalize_into(block, owned)
     loads[1].wait()
     loads[2].wait()
-    real, imag = spectra_of(block, padded.at[pl.ds(0, SOURCES * WIN)], tables)
+    real, imag = spectra_of(owned, tables)
     for s in range(SOURCES):
         local = ids[s % 2, s // 2] - base
         mine = jnp.logical_and(local >= 0, local < channels).astype(jnp.float32)
@@ -211,7 +230,8 @@
 
     def spectra_to_near(places):
         block = jnp.concatenate([records[lo:hi] for lo, hi in places], axis=0)
-        real, imag = spectra_of(block.reshape(-1, L), padded, tables)
+        normalize_into(block.reshape(-1, L), padded)
+        real, imag = spectra_of(padded, tables)
         row = 0
         for lo, hi in places:
             size = hi - lo
@@ -230,8 +250,10 @@
 
     ka, kb = slots(ys), slots(zs)
     first = start(
-        [remote(ka + d, half.at[pl.ds(0, group), to(d, y, ys)], ra1.at[d - 1], at_y(d)) for d in range(1, ys)]
-        + [remote(kb + d, half.at[pl.ds(group, group), to(d, z, zs)], rb1.at[d - 1], at_z(d)) for d in range(1, zs)])
+        [c for d in y_far for c in (
+            remote(ka + d, half.at[pl.ds(0, group), to(d, y, ys)], ra1.at[d - 1], at_y(d)),
+            remote(kb + d, half.at[pl.ds(group, group), to(d, z, zs)], rb1.at[d - 1], at_z(d)))])
+    loads[3].start()
 
     spectra_to_near([(0, NEAR), (channels - NEAR, channels)])
     k = slots(2)
@@ -240,7 +262,7 @@
         remote(k + 1, near.at[pl.ds(NEAR, NEAR)], near.at[pl.ds(NEAR + channels, NEAR)], before)])
     spectra_to_near([(NEAR, channels - NEAR)])
     turned = [
-        pltpu.make_async_copy(near.at[pl.ds(NEAR, channels), w], by_window.at[w], load.at[len(loads) + w])
+        pltpu.make_async_copy(near.at[pl.ds(NEAR, channels), w], by_window.at[w], load.at[7 + w])
         for w in range(WIN)
     ]
     for c in turned:
@@ -251,15 +273,17 @@
     piece[1] = half[group:, pl.ds(z * span, span)] + sum(rb1[d] for d in range(zs - 1))
     ka, kb = slots(zs), slots(ys)
     second = start(
-        [remote(ka + d, piece.at[0], ra2.at[d - 1], at_z(d)) for d in range(1, zs)]
-        + [remote(kb + d, piece.at[1], rb2.at[d - 1], at_y(d)) for d in range(1, ys)])
+        [c for d in y_far for c in (
+            remote(ka + d, piece.at[0], ra2.at[d - 1], at_z(d)),
+            remote(kb + d, piece.at[1], rb2.at[d - 1], at_y(d)))])
     arrive(second)
     piece[2] = piece[0] + sum(ra2[d] for d in range(zs - 1))
     piece[3] = piece[1] + sum(rb2[d] for d in range(ys - 1))
     k = slots(xs)
-    third = start([remote(k + d, piece.at[pl.ds(2, 2)], r3.at[d - 1], at_x(d)) for d in range(1, xs)])
+    third = start([remote(k + d, piece.at[pl.ds(2, 2)], r3.at[d - 1], at_x(d)) for d in x_far])
 
     arrive(halo)
+    numbers[1].wait()
     slot_count = pair_cross.shape[0]
 
     def one_pair(slot, carry):
@@ -301,11 +325,12 @@
         got = block_b(own, lax.rem(z + zs - d, zs))
         return remote(fb + d, got, got, sibling)
 
-    fourth = start([g(d) for d in range(1, ys) for g in (gather_a, gather_b)])
+    fourth = start([g(d) for d in y_far for g in (gather_a, gather_b)])
     start([pass_a(0), pass_b(0)])
 
     for c in loads[3:] + turned:
         c.wait()
+    numbers[2].wait()
     result = dot3(pair_cross[...], tables[LAG_AT:, :LAGS], tables[LAG_AT:, LAGS:])
     live = lax.broadcasted_iota(jnp.int32, (slot_count, 1), 0) < count[0]
     pair_res[...] = result * live.astype(jnp.float32)
@@ -363,11 +388,28 @@
     store_other.wait()
 
 
+def deliver(source_in, pair_in, source_out, pair_out, source_held, pair_held, sems):
+    inward, outward = [], []
+    for src, held, dst in ((source_in, source_held, source_out), (pair_in, pair_held, pair_out)):
+        rows = src.shape[0] // PARTS
+        for p in range(PARTS):
+            part = pl.ds(p * rows, rows)
+            k = len(inward)
+            inward.append(pltpu.make_async_copy(src.at[part], held.at[part], sems.at[0, k]))
+            outward.append(pltpu.make_async_copy(held.at[part], dst.at[part], sems.at[1, k]))
+    for c in inward:
+        c.start()
+    for c, o in zip(inward, outward):
+        c.wait()
+        o.start()
+    for o in outward:
+        o.wait()
+
+
 def shards(dims, das_records, source_ids, near_pairs, pair_count):
     xs, ys, zs = dims
     channels = das_records.shape[0]
     slot_count = near_pairs.shape[0]
-    smem = pl.BlockSpec(memory_space=pltpu.SMEM)
     hbm = pl.BlockSpec(memory_space=pl.ANY)
     f32 = jnp.float32
     per_core = SOURCES // CORES
@@ -383,7 +425,7 @@
             jax.ShapeDtypeStruct((CORES, per_core * channels, LAGS), f32),
             jax.ShapeDtypeStruct((slot_count, LAGS), f32),
         ),
-        in_specs=[smem, smem, smem, hbm, hbm],
+        in_specs=[hbm, hbm, hbm, hbm, hbm],
         out_specs=(hbm, hbm),
         scratch_shapes=[
             pltpu.VMEM(das_records.shape, f32),
@@ -405,7 +447,10 @@
             pltpu.VMEM((slot_count, 2 * NB), f32),
             pltpu.VMEM((CORES, per_core * channels, LAGS), f32),
             pltpu.VMEM((slot_count, LAGS), f32),
-            pltpu.SemaphoreType.DMA((4 + WIN,)),
+            pltpu.SMEM(source_ids.shape[::-1], jnp.int32),
+            pltpu.SMEM(near_pairs.shape[::-1], jnp.int32),
+            pltpu.SMEM(pair_count.shape, jnp.int32),
+            pltpu.SemaphoreType.DMA((7 + WIN,)),
             pltpu.SemaphoreType.DMA((n_copies,)),
             pltpu.SemaphoreType.DMA((n_copies,)),
         ],
@@ -413,6 +458,22 @@
             collective_id=0, has_side_effects=True, vmem_limit_bytes=VMEM_LIMIT),
         name="correlate_all",
     )(source_ids.T, near_pairs.T, pair_count, das_records, jnp.asarray(tables))
+    source_xcorr, pair_xcorr = pl.pallas_call(
+        deliver,
+        out_shape=(
+            jax.ShapeDtypeStruct(source_xcorr.shape, f32),
+            jax.ShapeDtypeStruct(pair_xcorr.shape, f32),
+        ),
+        in_specs=[hbm, hbm],
+        out_specs=(hbm, hbm),
+        scratch_shapes=[
+            pltpu.VMEM(source_xcorr.shape, f32),
+            pltpu.VMEM(pair_xcorr.shape, f32),
+            pltpu.SemaphoreType.DMA((2, 2 * PARTS)),
+        ],
+        compiler_params=pltpu.CompilerParams(vmem_limit_bytes=VMEM_LIMIT),
+        name="deliver",
+    )(source_xcorr, pair_xcorr)
     return source_xcorr.reshape(source_ids.shape + (channels, LAGS)), pair_xcorr
 
 

time: 49.7 us -> 47.1 us (0.948)
  local copies, waits for them, and re-layouts: 3.24 us -> 0 us
  Pallas kernels: 45 us -> 45.7 us
    unnamed x2 -> x0, local copies, waits for them, and re-layouts: 3.24 us -> none
    pallas_call x0 -> x1, Pallas kernels: none -> 1.73 us  [shards(): pl.pallas_call(deliver, out_shape=(jax.ShapeDtypeStruct(source_xcorr.shap...]
    pallas_call x1, Pallas kernels: 45 us -> 43.9 us  [shards(): pl.pallas_call(functools.partial(kernel, dims), out_shape=(jax.ShapeDtype...]
where the time goes in v3:
time: 47.1 us; the launch traced here: 47 us
  Pallas kernels  45.7 us (97%)
  between operations  1.29 us (3%)
    pallas_call x1, Pallas kernels, shards(): pl.pallas_call(functools.partial(kernel, dims), out_shape=(jax.ShapeDtype...  43.9 us
    pallas_call x1, Pallas kernels, shards(): pl.pallas_call(deliver, out_shape=(jax.ShapeDtypeStruct(source_xcorr.shap...  1.73 us

profile of v3, /device:TPU:1, one launch (start us, length us, event | category | flops | bytes accessed | tf_op | source)
XLA Modules:
  0.0 47.0 jit_solution(6289266599698334764)
XLA Ops:
  1.3 43.9 %correlate_all.1 = (f32[2,128,256]{2,1,0:T(8,128)}, f32[128,256]{1,0:T(8,128)}) custom-call(s32[2,4]{1,0:T(2,128)} %bitcast.3, s32[2,128]{1,0:T(2,128)} %bitcast.4, s32[1]{0:T(128)S(6)} %copy.7.count_hbm, f32[32,8,1500]{2,1,0:T(8,128)} %records_hbm.1, bf16[4608,512]{1,0:T(8,128)(2,1)} %constant.2.clone.tables_hbm), custom_call_target="tpu_custom_call" | custom-call | tf_op jit(solution)/shard_map/correlate_all/pallas_call | solution.py:422
  45.2 1.7 %deliver.1 = (f32[2,128,256]{2,1,0:T(8,128)}, f32[128,256]{1,0:T(8,128)}) custom-call(f32[2,128,256]{2,1,0:T(8,128)} %get-tuple-element.6.source_in, f32[128,256]{1,0:T(8,128)} %get-tuple-element.7.pair_in), custom_call_target="tpu_custom_call" | custom-call | tf_op jit(solution)/shard_map/deliver/pallas_call | solution.py:461

commit v4 on v3

--- a/solution.py
+++ b/solution.py
@@ -157,6 +157,9 @@
     def at_x(d):
         return at(z, core, y, lax.rem(x + d, xs))
 
+    def at_x_other(d):
+        return at(z, 1 - core, y, lax.rem(x + d, xs))
+
     def at_y(d):
         return at(z, core, lax.rem(y + d, ys), x)
 
@@ -170,7 +173,7 @@
     barrier = pltpu.get_barrier_semaphore()
     y_far, x_far = far_first(ys), far_first(xs)
     greeted = [there(d) for d in y_far for there in (at_y, at_z)]
-    greeted += [at_x(d) for d in x_far] + [after, before, sibling]
+    greeted += [there(d) for d in x_far for there in (at_x, at_x_other)] + [after, before, sibling]
     for device in greeted:
         pl.semaphore_signal(barrier, inc=1, device_id=device, device_id_type=MESH)
 
@@ -279,8 +282,12 @@
     arrive(second)
     piece[2] = piece[0] + sum(ra2[d] for d in range(zs - 1))
     piece[3] = piece[1] + sum(rb2[d] for d in range(ys - 1))
-    k = slots(xs)
-    third = start([remote(k + d, piece.at[pl.ds(2, 2)], r3.at[d - 1], at_x(d)) for d in x_far])
+    k = slots(2 * xs)
+    summed = piece.at[pl.ds(2, 2)]
+    third = start(
+        [c for d in x_far for c in (
+            remote(k + xs + d, summed, r3.at[1, d], at_x_other(d)), remote(k + d, summed, r3.at[0, d], at_x(d)))]
+        + [remote(k + xs, summed, r3.at[1, 0], sibling)])
 
     arrive(halo)
     numbers[1].wait()
@@ -297,36 +304,20 @@
     lax.fori_loop(0, slot_count, one_pair, 0, unroll=4)
 
     arrive(third)
-    whole = piece[2:] + sum(r3[d] for d in range(xs - 1))
-    own = core * per_core
-    other = (1 - core) * per_core
-    sources[pl.ds(own, group), pl.ds(y * span, span)] = whole[0]
-    sources[pl.ds(own + group, group), pl.ds(z * span, span)] = whole[1]
-
-    def block_a(owner, origin):
-        return sources.at[pl.ds(owner, group), pl.ds(origin * span, span)]
-
-    def block_b(owner, origin):
-        return sources.at[pl.ds(owner + group, group), pl.ds(origin * span, span)]
-
-    ka, kb, fa, fb = slots(ys), slots(zs), slots(ys), slots(zs)
+    for c, whole in ((core, piece[2:] + sum(r3[0, d] for d in range(1, xs))), (1 - core, sum(r3[1, d] for d in range(xs)))):
+        sources[c, 0, :, pl.ds(y * span, span)] = whole[0]
+        sources[c, 1, :, pl.ds(z * span, span)] = whole[1]
+    ka, kb = slots(ys), slots(zs)
 
     def gather_a(d):
-        return remote(ka + d, block_a(own, y), block_a(own, y), at_y(d))
+        block = sources.at[:, 0, :, pl.ds(y * span, span)]
+        return remote(ka + d, block, block, at_y(d))
 
     def gather_b(d):
-        return remote(kb + d, block_b(own, z), block_b(own, z), at_z(d))
-
-    def pass_a(d):
-        got = block_a(own, lax.rem(y + ys - d, ys))
-        return remote(fa + d, got, got, sibling)
-
-    def pass_b(d):
-        got = block_b(own, lax.rem(z + zs - d, zs))
-        return remote(fb + d, got, got, sibling)
+        block = sources.at[:, 1, :, pl.ds(z * span, span)]
+        return remote(kb + d, block, block, at_z(d))
 
     fourth = start([g(d) for d in y_far for g in (gather_a, gather_b)])
-    start([pass_a(0), pass_b(0)])
 
     for c in loads[3:] + turned:
         c.wait()
@@ -337,55 +328,48 @@
     pair_store = pltpu.make_async_copy(pair_res, pair_out, load.at[0])
     pair_store.start()
 
-    def add_window(s, w):
+    def add_window(c, h, g, w):
+        s = (c * 2 + h) * group + g
         for t in range(ROWS // 2):
-            s_re = sources[s, w, t : t + 1]
-            s_im = sources[s, w, ROWS // 2 + t : ROWS // 2 + t + 1]
+            s_re = sources[c, h, g, w, t : t + 1]
+            s_im = sources[c, h, g, w, ROWS // 2 + t : ROWS // 2 + t + 1]
             re, im = slice(t * LANES, (t + 1) * LANES), slice(NB + t * LANES, NB + (t + 1) * LANES)
             c_re = by_window[w, :, re]
             c_im = by_window[w, :, im]
             acc[s, :, re] += s_re * c_re + s_im * c_im
             acc[s, :, im] += s_re * c_im - s_im * c_re
 
-    def add_blocks(owner, d):
-        for g in range(group):
-            for v in range(span):
-                add_window(owner + g, lax.rem(y + ys - d, ys) * span + v)
-                add_window(owner + group + g, lax.rem(z + zs - d, zs) * span + v)
+    def add_blocks(d):
+        for v in range(span):
+            for h, w in enumerate((lax.rem(y + ys - d, ys) * span + v, lax.rem(z + zs - d, zs) * span + v)):
+                for c in range(CORES):
+                    for g in range(group):
+                        add_window(c, h, g, w)
 
     def nth(i):
         return jnp.where(lax.rem(i, 2) == 1, (i + 1) // 2, lax.rem(ys - i // 2, ys))
 
-    add_blocks(own, 0)
+    add_blocks(0)
 
     def step(i, carry):
-        d, previous = nth(i), nth(i - 1)
+        d = nth(i)
         gather_a(d).wait_recv()
-        pass_a(d).start()
         gather_b(d).wait_recv()
-        pass_b(d).start()
-        add_blocks(own, d)
-        pass_a(previous).wait_recv()
-        pass_b(previous).wait_recv()
-        add_blocks(other, previous)
+        add_blocks(d)
         return carry
 
     lax.fori_loop(1, ys, step, 0)
-    source_res[0] = dot3(acc[pl.ds(own, per_core)].reshape(per_core * channels, 2 * NB), tables[LAG_AT:, :LAGS], tables[LAG_AT:, LAGS:])
-    store_own = pltpu.make_async_copy(source_res.at[0], source_out.at[own // per_core], load.at[1])
-    store_own.start()
-    last = ys // 2
-    pass_a(last).wait_recv()
-    pass_b(last).wait_recv()
-    add_blocks(other, last)
-    source_res[1] = dot3(acc[pl.ds(other, per_core)].reshape(per_core * channels, 2 * NB), tables[LAG_AT:, :LAGS], tables[LAG_AT:, LAGS:])
-    store_other = pltpu.make_async_copy(source_res.at[1], source_out.at[other // per_core], load.at[2])
-    store_other.start()
-    for c in core_copy + first + halo + second + third + fourth + [p(d) for d in range(ys) for p in (pass_a, pass_b)]:
+    stores = []
+    for c in range(CORES):
+        mine = acc[c * per_core : (c + 1) * per_core].reshape(per_core * channels, 2 * NB)
+        source_res[c] = dot3(mine, tables[LAG_AT:, :LAGS], tables[LAG_AT:, LAGS:])
+        stores.append(pltpu.make_async_copy(source_res.at[c], source_out.at[c], load.at[1 + c]))
+        stores[c].start()
+    for c in core_copy + first + halo + second + third + fourth:
         c.wait_send()
     pair_store.wait()
-    store_own.wait()
-    store_other.wait()
+    for c in stores:
+        c.wait()
 
 
 def deliver(source_in, pair_in, source_out, pair_out, source_held, pair_held, sems):
@@ -418,7 +402,7 @@
     tables = all_tables()
     tile = (ROWS, LANES)
     block = (group, span) + tile
-    n_copies = 3 + 4 * ys + 4 * zs + xs
+    n_copies = 3 + 3 * ys + 3 * zs + 2 * xs
     source_xcorr, pair_xcorr = pl.pallas_call(
         functools.partial(kernel, dims),
         out_shape=(
@@ -441,8 +425,8 @@
             pltpu.VMEM((zs - 1,) + block, f32),
             pltpu.VMEM((ys - 1,) + block, f32),
             pltpu.VMEM((4,) + block, f32),
-            pltpu.VMEM((xs - 1, 2) + block, f32),
-            pltpu.VMEM((SOURCES, WIN) + tile, f32),
+            pltpu.VMEM((2, xs, 2) + block, f32),
+            pltpu.VMEM((CORES, 2, group, WIN) + tile, f32),
             pltpu.VMEM((SOURCES, channels, 2 * NB), f32),
             pltpu.VMEM((slot_count, 2 * NB), f32),
             pltpu.VMEM((CORES, per_core * channels, LAGS), f32),

time: 47.1 us -> 44.5 us (0.945)
  Pallas kernels: 45.7 us -> 43.1 us
    pallas_call x1, Pallas kernels: 43.9 us -> 41.4 us  [shards(): pl.pallas_call(functools.partial(kernel, dims), out_shape=(jax.ShapeDtype...]
where the time goes in v4:
time: 44.5 us; the launch traced here: 44.4 us
  Pallas kernels  43.1 us (97%)
  between operations  1.29 us (3%)
    pallas_call x1, Pallas kernels, shards(): pl.pallas_call(functools.partial(kernel, dims), out_shape=(jax.ShapeDtype...  41.4 us
    pallas_call x1, Pallas kernels, shards(): pl.pallas_call(deliver, out_shape=(jax.ShapeDtypeStruct(source_xcorr.shap...  1.73 us

profile of v4, /device:TPU:1, one launch (start us, length us, event | category | flops | bytes accessed | tf_op | source)
XLA Modules:
  0.0 44.4 jit_solution(6155802644661047966)
XLA Ops:
  1.3 41.4 %correlate_all.1 = (f32[2,128,256]{2,1,0:T(8,128)}, f32[128,256]{1,0:T(8,128)}) custom-call(s32[2,4]{1,0:T(2,128)} %bitcast.3, s32[2,128]{1,0:T(2,128)} %bitcast.4, s32[1]{0:T(128)S(6)} %copy.7.count_hbm, f32[32,8,1500]{2,1,0:T(8,128)} %records_hbm.1, bf16[4608,512]{1,0:T(8,128)(2,1)} %constant.2.clone.tables_hbm), custom_call_target="tpu_custom_call" | custom-call | tf_op jit(solution)/shard_map/correlate_all/pallas_call | solution.py:406
  42.7 1.7 %deliver.1 = (f32[2,128,256]{2,1,0:T(8,128)}, f32[128,256]{1,0:T(8,128)}) custom-call(f32[2,128,256]{2,1,0:T(8,128)} %get-tuple-element.6.source_in, f32[128,256]{1,0:T(8,128)} %get-tuple-element.7.pair_in), custom_call_target="tpu_custom_call" | custom-call | tf_op jit(solution)/shard_map/deliver/pallas_call | solution.py:445

commit v5 on v4

--- a/solution.py
+++ b/solution.py
@@ -259,10 +259,16 @@
     loads[3].start()
 
     spectra_to_near([(0, NEAR), (channels - NEAR, channels)])
-    k = slots(2)
-    halo = start([
-        remote(k, near.at[pl.ds(channels, NEAR)], near.at[pl.ds(0, NEAR)], after),
-        remote(k + 1, near.at[pl.ds(NEAR, NEAR)], near.at[pl.ds(NEAR + channels, NEAR)], before)])
+    k_halo = slots(4)
+
+    def halo_part(p):
+        size = NEAR // 2
+        up, down = channels + p * size, NEAR + p * size
+        return start([
+            remote(k_halo + 2 * p, near.at[pl.ds(up, size)], near.at[pl.ds(up - channels, size)], after),
+            remote(k_halo + 2 * p + 1, near.at[pl.ds(down, size)], near.at[pl.ds(down + channels, size)], before)])
+
+    halo = halo_part(0)
     spectra_to_near([(NEAR, channels - NEAR)])
     turned = [
         pltpu.make_async_copy(near.at[pl.ds(NEAR, channels), w], by_window.at[w], load.at[7 + w])
@@ -279,6 +285,7 @@
         [c for d in y_far for c in (
             remote(ka + d, piece.at[0], ra2.at[d - 1], at_z(d)),
             remote(kb + d, piece.at[1], rb2.at[d - 1], at_y(d)))])
+    halo += halo_part(1)
     arrive(second)
     piece[2] = piece[0] + sum(ra2[d] for d in range(zs - 1))
     piece[3] = piece[1] + sum(rb2[d] for d in range(ys - 1))
@@ -328,37 +335,37 @@
     pair_store = pltpu.make_async_copy(pair_res, pair_out, load.at[0])
     pair_store.start()
 
-    def add_window(c, h, g, w):
-        s = (c * 2 + h) * group + g
-        for t in range(ROWS // 2):
-            s_re = sources[c, h, g, w, t : t + 1]
-            s_im = sources[c, h, g, w, ROWS // 2 + t : ROWS // 2 + t + 1]
-            re, im = slice(t * LANES, (t + 1) * LANES), slice(NB + t * LANES, NB + (t + 1) * LANES)
-            c_re = by_window[w, :, re]
-            c_im = by_window[w, :, im]
-            acc[s, :, re] += s_re * c_re + s_im * c_im
-            acc[s, :, im] += s_re * c_im - s_im * c_re
-
-    def add_blocks(d):
-        for v in range(span):
-            for h, w in enumerate((lax.rem(y + ys - d, ys) * span + v, lax.rem(z + zs - d, zs) * span + v)):
+    def add_blocks(*distances):
+        for h, (mine, n) in enumerate(((y, ys), (z, zs))):
+            windows = [lax.rem(mine + n - d, n) * span + v for d in distances for v in range(span)]
+            for t in range(ROWS // 2):
+                re, im = slice(t * LANES, (t + 1) * LANES), slice(NB + t * LANES, NB + (t + 1) * LANES)
+                local = [(by_window[w, :, re], by_window[w, :, im]) for w in windows]
                 for c in range(CORES):
                     for g in range(group):
-                        add_window(c, h, g, w)
-
-    def nth(i):
-        return jnp.where(lax.rem(i, 2) == 1, (i + 1) // 2, lax.rem(ys - i // 2, ys))
+                        s = (c * 2 + h) * group + g
+                        sum_re, sum_im = acc[s, :, re], acc[s, :, im]
+                        for w, (c_re, c_im) in zip(windows, local):
+                            s_re = sources[c, h, g, w, t : t + 1]
+                            s_im = sources[c, h, g, w, ROWS // 2 + t : ROWS // 2 + t + 1]
+                            sum_re += s_re * c_re + s_im * c_im
+                            sum_im += s_re * c_im - s_im * c_re
+                        acc[s, :, re] = sum_re
+                        acc[s, :, im] = sum_im
 
     add_blocks(0)
 
     def step(i, carry):
-        d = nth(i)
-        gather_a(d).wait_recv()
-        gather_b(d).wait_recv()
-        add_blocks(d)
+        for d in (i, ys - i):
+            gather_a(d).wait_recv()
+            gather_b(d).wait_recv()
+        add_blocks(i, ys - i)
         return carry
 
-    lax.fori_loop(1, ys, step, 0)
+    lax.fori_loop(1, ys // 2, step, 0)
+    gather_a(ys // 2).wait_recv()
+    gather_b(ys // 2).wait_recv()
+    add_blocks(ys // 2)
     stores = []
     for c in range(CORES):
         mine = acc[c * per_core : (c + 1) * per_core].reshape(per_core * channels, 2 * NB)
@@ -402,7 +409,7 @@
     tables = all_tables()
     tile = (ROWS, LANES)
     block = (group, span) + tile
-    n_copies = 3 + 3 * ys + 3 * zs + 2 * xs
+    n_copies = 5 + 3 * ys + 3 * zs + 2 * xs
     source_xcorr, pair_xcorr = pl.pallas_call(
         functools.partial(kernel, dims),
         out_shape=(

time: 44.5 us -> 43.9 us (0.987)
  Pallas kernels: 43.1 us -> 42.5 us
    pallas_call x1, Pallas kernels: 41.4 us -> 40.7 us  [shards(): pl.pallas_call(functools.partial(kernel, dims), out_shape=(jax.ShapeDtype...]
where the time goes in v5:
time: 43.9 us; the launch traced here: 43.7 us
  Pallas kernels  42.5 us (97%)
  between operations  1.29 us (3%)
    pallas_call x1, Pallas kernels, shards(): pl.pallas_call(functools.partial(kernel, dims), out_shape=(jax.ShapeDtype...  40.7 us
    pallas_call x1, Pallas kernels, shards(): pl.pallas_call(deliver, out_shape=(jax.ShapeDtypeStruct(source_xcorr.shap...  1.73 us

profile of v5, /device:TPU:1, one launch (start us, length us, event | category | flops | bytes accessed | tf_op | source)
XLA Modules:
  0.0 43.7 jit_solution(16506930095023856046)
XLA Ops:
  1.3 40.7 %correlate_all.1 = (f32[2,128,256]{2,1,0:T(8,128)}, f32[128,256]{1,0:T(8,128)}) custom-call(s32[2,4]{1,0:T(2,128)} %bitcast.3, s32[2,128]{1,0:T(2,128)} %bitcast.4, s32[1]{0:T(128)S(6)} %copy.7.count_hbm, f32[32,8,1500]{2,1,0:T(8,128)} %records_hbm.1, bf16[4608,512]{1,0:T(8,128)(2,1)} %constant.2.clone.tables_hbm), custom_call_target="tpu_custom_call" | custom-call | tf_op jit(solution)/shard_map/correlate_all/pallas_call | solution.py:413
  42.0 1.7 %deliver.1 = (f32[2,128,256]{2,1,0:T(8,128)}, f32[128,256]{1,0:T(8,128)}) custom-call(f32[2,128,256]{2,1,0:T(8,128)} %get-tuple-element.6.source_in, f32[128,256]{1,0:T(8,128)} %get-tuple-element.7.pair_in), custom_call_target="tpu_custom_call" | custom-call | tf_op jit(solution)/shard_map/deliver/pallas_call | solution.py:452

commit v6 on v5

--- a/solution.py
+++ b/solution.py
@@ -191,7 +191,6 @@
 
     tail = padded.shape[0]
     padded[:, LPAD - LANES :] = jnp.zeros((tail, LANES), jnp.float32)
-    acc[...] = jnp.zeros_like(acc)
 
     numbers[0].wait()
     loads[0].wait()
@@ -257,6 +256,7 @@
             remote(ka + d, half.at[pl.ds(0, group), to(d, y, ys)], ra1.at[d - 1], at_y(d)),
             remote(kb + d, half.at[pl.ds(group, group), to(d, z, zs)], rb1.at[d - 1], at_z(d)))])
     loads[3].start()
+    acc[...] = jnp.zeros_like(acc)
 
     spectra_to_near([(0, NEAR), (channels - NEAR, channels)])
     k_halo = slots(4)

time: 43.9 us -> 44 us (level)
  no operation moved by 1% of the time
where the time goes in v6:
time: 44 us; the launch traced here: 43.9 us
  Pallas kernels  42.6 us (97%)
  between operations  1.29 us (3%)
    pallas_call x1, Pallas kernels, shards(): pl.pallas_call(functools.partial(kernel, dims), out_shape=(jax.ShapeDtype...  40.9 us
    pallas_call x1, Pallas kernels, shards(): pl.pallas_call(deliver, out_shape=(jax.ShapeDtypeStruct(source_xcorr.shap...  1.73 us

profile of v6, /device:TPU:1, one launch (start us, length us, event | category | flops | bytes accessed | tf_op | source)
XLA Modules:
  0.0 43.9 jit_solution(15149886240306251827)
XLA Ops:
  1.3 40.9 %correlate_all.1 = (f32[2,128,256]{2,1,0:T(8,128)}, f32[128,256]{1,0:T(8,128)}) custom-call(s32[2,4]{1,0:T(2,128)} %bitcast.3, s32[2,128]{1,0:T(2,128)} %bitcast.4, s32[1]{0:T(128)S(6)} %copy.7.count_hbm, f32[32,8,1500]{2,1,0:T(8,128)} %records_hbm.1, bf16[4608,512]{1,0:T(8,128)(2,1)} %constant.2.clone.tables_hbm), custom_call_target="tpu_custom_call" | custom-call | tf_op jit(solution)/shard_map/correlate_all/pallas_call | solution.py:413
  42.1 1.7 %deliver.1 = (f32[2,128,256]{2,1,0:T(8,128)}, f32[128,256]{1,0:T(8,128)}) custom-call(f32[2,128,256]{2,1,0:T(8,128)} %get-tuple-element.6.source_in, f32[128,256]{1,0:T(8,128)} %get-tuple-element.7.pair_in), custom_call_target="tpu_custom_call" | custom-call | tf_op jit(solution)/shard_map/deliver/pallas_call | solution.py:452

commit v7 on v6

--- a/solution.py
+++ b/solution.py
@@ -366,10 +366,10 @@
     gather_a(ys // 2).wait_recv()
     gather_b(ys // 2).wait_recv()
     add_blocks(ys // 2)
+    lagged = dot3(acc[...].reshape(SOURCES * channels, 2 * NB), tables[LAG_AT:, :LAGS], tables[LAG_AT:, LAGS:])
     stores = []
     for c in range(CORES):
-        mine = acc[c * per_core : (c + 1) * per_core].reshape(per_core * channels, 2 * NB)
-        source_res[c] = dot3(mine, tables[LAG_AT:, :LAGS], tables[LAG_AT:, LAGS:])
+        source_res[c] = lagged[c * per_core * channels : (c + 1) * per_core * channels]
         stores.append(pltpu.make_async_copy(source_res.at[c], source_out.at[c], load.at[1 + c]))
         stores[c].start()
     for c in core_copy + first + halo + second + third + fourth:

time: 44 us -> 44 us (level)
  no operation moved by 1% of the time
where the time goes in v7:
time: 44 us; the launch traced here: 43.8 us
  Pallas kernels  42.5 us (97%)
  between operations  1.29 us (3%)
    pallas_call x1, Pallas kernels, shards(): pl.pallas_call(functools.partial(kernel, dims), out_shape=(jax.ShapeDtype...  40.8 us
    pallas_call x1, Pallas kernels, shards(): pl.pallas_call(deliver, out_shape=(jax.ShapeDtypeStruct(source_xcorr.shap...  1.73 us

profile of v7, /device:TPU:1, one launch (start us, length us, event | category | flops | bytes accessed | tf_op | source)
XLA Modules:
  0.0 43.8 jit_solution(15353615348228760491)
XLA Ops:
  1.3 40.8 %correlate_all.1 = (f32[2,128,256]{2,1,0:T(8,128)}, f32[128,256]{1,0:T(8,128)}) custom-call(s32[2,4]{1,0:T(2,128)} %bitcast.3, s32[2,128]{1,0:T(2,128)} %bitcast.4, s32[1]{0:T(128)S(6)} %copy.7.count_hbm, f32[32,8,1500]{2,1,0:T(8,128)} %records_hbm.1, bf16[4608,512]{1,0:T(8,128)(2,1)} %constant.2.clone.tables_hbm), custom_call_target="tpu_custom_call" | custom-call | tf_op jit(solution)/shard_map/correlate_all/pallas_call | solution.py:413
  42.1 1.7 %deliver.1 = (f32[2,128,256]{2,1,0:T(8,128)}, f32[128,256]{1,0:T(8,128)}) custom-call(f32[2,128,256]{2,1,0:T(8,128)} %get-tuple-element.6.source_in, f32[128,256]{1,0:T(8,128)} %get-tuple-element.7.pair_in), custom_call_target="tpu_custom_call" | custom-call | tf_op jit(solution)/shard_map/deliver/pallas_call | solution.py:452
